TPU v7x, 32 devices: a whole 2x2x4 slice. The times are simulated.
32 devices in a mesh: shard: 8 (over y, x, core), seq: 4 (over z).
Axes of the slice: x: 2, y: 2, z: 4, core: 2. Of those that a mesh axis runs over, the one named last changes fastest.
Arguments:
- tokens: bfloat16 [8, 28, 112, 512], P('shard', 'seq'), may hold values from -6 to 6
- regions: int32 [8, 28, 112], P('shard'), may hold values from 0 to 8, as said below
- cotangent: bfloat16 [8, 28, 112, 512], P('shard', 'seq'), may hold values from -6 to 6
- gain_one: bfloat16 [512], P('shard'), may hold values from 0.5 to 1.5
- bias_one: bfloat16 [512], P('shard'), may hold values from -1 to 1
- w_qkv: bfloat16 [512, 1536], P('shard'), may hold values from -0.25 to 0.25
- bias_qv: bfloat16 [2, 512], P(None, 'shard'), may hold values from -1 to 1
- table: bfloat16 [169, 16], P(None, 'shard'), may hold values from -4 to 4
- w_proj: bfloat16 [512, 512], P('shard'), may hold values from -1 to 1
- bias_proj: bfloat16 [512], P('shard'), may hold values from -1 to 1
- gain_two: bfloat16 [512], P('shard'), may hold values from 0.5 to 1.5
- bias_two: bfloat16 [512], P('shard'), may hold values from -1 to 1
- w_in: bfloat16 [512, 2048], P('shard'), may hold values from -0.25 to 0.25
- bias_in: bfloat16 [2048], P('shard'), may hold values from -1 to 1
- w_out: bfloat16 [2048, 512], P('shard'), may hold values from -0.125 to 0.125
- bias_out: bfloat16 [512], P('shard'), may hold values from -1 to 1
Outputs:
- output: float32 [8, 28, 112, 512], P('shard', 'seq')
- grad_tokens: float32 [8, 28, 112, 512], P('shard', 'seq')
- grad_gain_one: float32 [512], P('shard')
- grad_bias_one: float32 [512], P('shard')
- grad_w_qkv: float32 [512, 1536], P('shard')
- grad_bias_qv: float32 [2, 512], P(None, 'shard')
- grad_table: float32 [169, 16], P(None, 'shard')
- grad_w_proj: float32 [512, 512], P('shard')
- grad_bias_proj: float32 [512], P('shard')
- grad_gain_two: float32 [512], P('shard')
- grad_bias_two: float32 [512], P('shard')
- grad_w_in: float32 [512, 2048], P('shard')
- grad_bias_in: float32 [2048], P('shard')
- grad_w_out: float32 [2048, 512], P('shard')
- grad_bias_out: float32 [512], P('shard')
Inputs may be any that keep to these rules, and one draw needn't show every extreme that they name: `regions`: tokens of one window attend to each other only where their labels are equal.
All inputs are finite; a program needn't handle non-finite values.
Results may differ from a plain program's by a relative error of at most 0.019.
Values may be sent and summed in bfloat16 or wider, within the bound.
No kernel may reach another device: no remote copies, remote signals or barrier semaphores. Data moves between devices by JAX's collectives and lax.ppermute only.
A program may use at most 128 MiB of HBM per device.

v0:
```python
import jax
import jax.numpy as jnp
from jax import lax
from jax.sharding import PartitionSpec as P

D = 512
HEADS = 16
HEAD = 32
WIN = 7
SHIFT = 3


EPS = 1e-05


def shifted_2(value, axis, by):
    peers = lax.axis_size(axis)
    return lax.ppermute(value, axis, [(i, (i + by) % peers) for i in range(peers)])


def normalize(values, gain, offset):
    average = jnp.mean(values, -1, keepdims=True)
    centered = values - average
    variance = jnp.mean(centered * centered, -1, keepdims=True)
    return centered * lax.rsqrt(variance + EPS) * gain + offset


def gelu_exact(values):
    return jax.nn.gelu(values, approximate=False)


def to_windows(tensor):
    images, height, columns, groups, depth = tensor.shape
    tensor = tensor.reshape(images, height // WIN, WIN, columns // WIN, WIN, groups, depth)
    return tensor.transpose(0, 1, 3, 5, 2, 4, 6).reshape(-1, groups, WIN * WIN, depth)


def from_windows(tensor, target):
    images, height, columns, groups, depth = target
    tensor = tensor.reshape(images, height // WIN, columns // WIN, groups, WIN, WIN, depth)
    return tensor.transpose(0, 1, 4, 2, 5, 3, 6).reshape(target)


def outer_sum(left, right):
    return lax.dot_general(
        left, right, (((0,), (0,)), ((), ())), preferred_element_type=jnp.float32
    )


def back_dot(left, right):
    return lax.dot_general(
        left, right, (((1,), (1,)), ((), ())), preferred_element_type=jnp.float32
    )


def penalty_of(labels_here):
    labels_win = to_windows(labels_here[:, :, :, None, None]).reshape(-1, WIN * WIN)
    return jnp.where(labels_win[:, :, None] != labels_win[:, None, :], -100.0, 0.0)[:, None]


def logits_of(query_win, key_win, penalty, rel_bias):
    scores = jnp.einsum("nhqe,nhke->nhqk", query_win, key_win, preferred_element_type=jnp.float32)
    return scores * HEAD ** (-0.5) + rel_bias[None] + penalty


def per_device(
    tokens,
    regions,
    cotangent,
    gain_one,
    bias_one,
    w_qkv,
    bias_qv,
    table,
    w_proj,
    bias_proj,
    gain_two,
    bias_two,
    w_in,
    bias_in,
    w_out,
    bias_out,
):
    images, local_rows, columns, features = tokens.shape
    tok_count = images * local_rows * columns
    seq_count = lax.axis_size("seq")
    seq_place = lax.axis_index("seq")
    gains_one, biases_one, qkv_weight, qv_bias, table_all, proj_weight, proj_bias = (
        lax.all_gather(gain_one, "shard", axis=0, tiled=True),
        lax.all_gather(bias_one, "shard", axis=0, tiled=True),
        lax.all_gather(w_qkv, "shard", axis=0, tiled=True),
        lax.all_gather(bias_qv, "shard", axis=1, tiled=True),
        lax.all_gather(table, "shard", axis=1, tiled=True),
        lax.all_gather(w_proj, "shard", axis=0, tiled=True),
        lax.all_gather(bias_proj, "shard", axis=0, tiled=True),
    )
    gains_two, biases_two, in_weight, in_bias, out_weight, out_bias = (
        lax.all_gather(gain_two, "shard", axis=0, tiled=True),
        lax.all_gather(bias_two, "shard", axis=0, tiled=True),
        lax.all_gather(w_in, "shard", axis=0, tiled=True),
        lax.all_gather(bias_in, "shard", axis=0, tiled=True),
        lax.all_gather(w_out, "shard", axis=0, tiled=True),
        lax.all_gather(bias_out, "shard", axis=0, tiled=True),
    )
    token_rows = tokens.astype(jnp.float32).reshape(tok_count, D)
    normed_one, norm_one_pull = jax.vjp(
        normalize, token_rows, gains_one.astype(jnp.float32), biases_one.astype(jnp.float32)
    )
    normed_low = normed_one.astype(jnp.bfloat16).reshape(images, local_rows, columns, D)
    upper_rows = shifted_2(normed_low[:, :SHIFT], "seq", -1)
    shifted = jnp.roll(
        jnp.concatenate([normed_low[:, SHIFT:], upper_rows], axis=1), -SHIFT, axis=2
    ).reshape(tok_count, D)
    projected = jnp.dot(shifted, qkv_weight, preferred_element_type=jnp.float32)
    qv_float = qv_bias.astype(jnp.float32)
    query_all = (projected[:, :D] + qv_float[0]).astype(jnp.bfloat16)
    key_all = projected[:, D : 2 * D].astype(jnp.bfloat16)
    value_all = (projected[:, 2 * D :] + qv_float[1]).astype(jnp.bfloat16)
    stacked = jnp.stack([query_all, key_all, value_all]).reshape(
        3, images, local_rows, columns, HEADS, HEAD
    )
    head_count = HEADS // seq_count
    arranged = lax.all_to_all(stacked, "seq", split_axis=4, concat_axis=2, tiled=True)
    bias_cols = lax.dynamic_slice_in_dim(table_all, seq_place * head_count, head_count, 1)
    target = arranged.shape[1:]
    position = jnp.arange(WIN * WIN, dtype=jnp.int32)
    pos_row = position // WIN
    pos_col = position % WIN
    relative = (
        (pos_row[:, None] - pos_row[None, :] + WIN - 1) * (2 * WIN - 1)
        + pos_col[:, None]
        - pos_col[None, :]
        + WIN
        - 1
    ).reshape(-1)
    selector = (
        relative[:, None] == jnp.arange(table_all.shape[0], dtype=jnp.int32)[None, :]
    ).astype(jnp.float32)
    rel_bias = jnp.dot(selector, bias_cols.astype(jnp.float32), precision=lax.Precision.HIGHEST)
    rel_bias = rel_bias.reshape(WIN * WIN, WIN * WIN, head_count).transpose(2, 0, 1)
    penalty = penalty_of(regions)
    query_win = to_windows(arranged[0])
    key_win = to_windows(arranged[1])
    value_win = to_windows(arranged[2])
    logits = logits_of(query_win, key_win, penalty, rel_bias)
    top_score = jnp.max(logits, -1, keepdims=True)
    log_total = top_score + jnp.log(jnp.sum(jnp.exp(logits - top_score), -1, keepdims=True))
    attention = jnp.exp(logits - log_total).astype(jnp.bfloat16)
    attended = jnp.einsum(
        "nhqk,nhke->nhqe", attention, value_win, preferred_element_type=jnp.float32
    ).astype(jnp.bfloat16)
    attended_tok = from_windows(attended, target)
    gathered_back = lax.all_to_all(attended_tok, "seq", split_axis=1, concat_axis=3, tiled=True)
    attended_rows = gathered_back.reshape(images, local_rows, columns, D)
    lower_rows = shifted_2(attended_rows[:, local_rows - SHIFT :], "seq", 1)
    restored = jnp.roll(
        jnp.concatenate([lower_rows, attended_rows[:, : local_rows - SHIFT]], axis=1), SHIFT, axis=2
    ).reshape(tok_count, D)
    mixed = token_rows + (
        jnp.dot(restored, proj_weight, preferred_element_type=jnp.float32)
        + proj_bias.astype(jnp.float32)
    )
    normed_two, norm_two_pull = jax.vjp(
        normalize, mixed, gains_two.astype(jnp.float32), biases_two.astype(jnp.float32)
    )
    normed_two_low = normed_two.astype(jnp.bfloat16)
    hidden = jnp.dot(
        normed_two_low, in_weight, preferred_element_type=jnp.float32
    ) + in_bias.astype(jnp.float32)
    activated, gelu_pull = jax.vjp(gelu_exact, hidden)
    activated_low = activated.astype(jnp.bfloat16)
    result = mixed + (
        jnp.dot(activated_low, out_weight, preferred_element_type=jnp.float32)
        + out_bias.astype(jnp.float32)
    )
    grad_low = cotangent.reshape(tok_count, D)
    grad_rows = grad_low.astype(jnp.float32)
    grad_out_bias = jnp.sum(grad_rows, 0)
    grad_out_weight = outer_sum(activated_low, grad_low)
    (grad_hidden,) = gelu_pull(back_dot(grad_low, out_weight))
    grad_hidden_low = grad_hidden.astype(jnp.bfloat16)
    grad_in_bias = jnp.sum(grad_hidden_low.astype(jnp.float32), 0)
    grad_in_weight = outer_sum(normed_two_low, grad_hidden_low)
    grad_mixed_norm, grad_gain_two, grad_bias_two = norm_two_pull(
        back_dot(grad_hidden_low, in_weight)
    )
    mlp_shares = (
        lax.psum_scatter(
            grad_gain_two.astype(jnp.bfloat16), "shard", scatter_dimension=0, tiled=True
        ).astype(jnp.float32),
        lax.psum_scatter(
            grad_bias_two.astype(jnp.bfloat16), "shard", scatter_dimension=0, tiled=True
        ).astype(jnp.float32),
        lax.psum_scatter(
            grad_in_weight.astype(jnp.bfloat16), "shard", scatter_dimension=0, tiled=True
        ).astype(jnp.float32),
        lax.psum_scatter(
            grad_in_bias.astype(jnp.bfloat16), "shard", scatter_dimension=0, tiled=True
        ).astype(jnp.float32),
        lax.psum_scatter(
            grad_out_weight.astype(jnp.bfloat16), "shard", scatter_dimension=0, tiled=True
        ).astype(jnp.float32),
        lax.psum_scatter(
            grad_out_bias.astype(jnp.bfloat16), "shard", scatter_dimension=0, tiled=True
        ).astype(jnp.float32),
    )
    grad_mixed = grad_rows + grad_mixed_norm
    grad_branch = grad_mixed.astype(jnp.bfloat16)
    grad_proj_bias = jnp.sum(grad_branch.astype(jnp.float32), 0)
    grad_proj_weight = outer_sum(restored, grad_branch)
    grad_restored = (
        back_dot(grad_branch, proj_weight)
        .astype(jnp.bfloat16)
        .reshape(images, local_rows, columns, D)
    )
    grad_rolled = jnp.roll(grad_restored, -SHIFT, axis=2)
    grad_upper = shifted_2(grad_rolled[:, :SHIFT], "seq", -1)
    grad_attended = jnp.concatenate([grad_rolled[:, SHIFT:], grad_upper], axis=1).reshape(
        images, local_rows, columns, HEADS, HEAD
    )
    grad_arranged = lax.all_to_all(grad_attended, "seq", split_axis=3, concat_axis=1, tiled=True)
    grad_win = to_windows(grad_arranged)
    logits_again = logits_of(query_win, key_win, penalty, rel_bias)
    attention_full = jnp.exp(logits_again - log_total)
    attention_low = attention_full.astype(jnp.bfloat16)
    grad_value = jnp.einsum(
        "nhqk,nhqe->nhke", attention_low, grad_win, preferred_element_type=jnp.float32
    ).astype(jnp.bfloat16)
    grad_attention = jnp.einsum(
        "nhqe,nhke->nhqk", grad_win, value_win, preferred_element_type=jnp.float32
    )
    inner_term = jnp.sum(attention_full * grad_attention, -1, keepdims=True)
    grad_logits = (attention_full * (grad_attention - inner_term)).astype(jnp.bfloat16)
    grad_query = (
        jnp.einsum("nhqk,nhke->nhqe", grad_logits, key_win, preferred_element_type=jnp.float32)
        * HEAD ** (-0.5)
    ).astype(jnp.bfloat16)
    grad_key = (
        jnp.einsum("nhqk,nhqe->nhke", grad_logits, query_win, preferred_element_type=jnp.float32)
        * HEAD ** (-0.5)
    ).astype(jnp.bfloat16)
    grad_rel = (
        jnp.sum(grad_logits.astype(jnp.float32), 0).transpose(1, 2, 0).reshape(WIN**4, head_count)
    )
    grad_table_here = lax.dot_general(
        selector,
        grad_rel,
        (((0,), (0,)), ((), ())),
        precision=lax.Precision.HIGHEST,
        preferred_element_type=jnp.float32,
    )
    grad_stacked = jnp.stack(
        [
            from_windows(grad_query, target),
            from_windows(grad_key, target),
            from_windows(grad_value, target),
        ]
    )
    grad_tokens_qkv = lax.all_to_all(grad_stacked, "seq", split_axis=2, concat_axis=4, tiled=True)
    grad_table_all = lax.dynamic_update_slice(
        jnp.zeros((table_all.shape[0], HEADS), jnp.float32),
        grad_table_here,
        (jnp.int32(0), seq_place * head_count),
    )
    grad_parts = grad_tokens_qkv.reshape(3, tok_count, D)
    grad_concat = jnp.concatenate([grad_parts[0], grad_parts[1], grad_parts[2]], axis=1)
    grad_qkv_weight = outer_sum(shifted, grad_concat)
    grad_qv_bias = jnp.stack(
        [
            jnp.sum(grad_parts[0].astype(jnp.float32), 0),
            jnp.sum(grad_parts[2].astype(jnp.float32), 0),
        ]
    )
    grad_shifted = (
        back_dot(grad_concat, qkv_weight)
        .astype(jnp.bfloat16)
        .reshape(images, local_rows, columns, D)
    )
    grad_unrolled = jnp.roll(grad_shifted, SHIFT, axis=2)
    grad_lower = shifted_2(grad_unrolled[:, local_rows - SHIFT :], "seq", 1)
    grad_normed = (
        jnp.concatenate([grad_lower, grad_unrolled[:, : local_rows - SHIFT]], axis=1)
        .reshape(tok_count, D)
        .astype(jnp.float32)
    )
    grad_token_norm, grad_gain_one, grad_bias_one = norm_one_pull(grad_normed)
    grad_inputs = grad_mixed + grad_token_norm
    attn_shares = (
        lax.psum_scatter(
            grad_gain_one.astype(jnp.bfloat16), "shard", scatter_dimension=0, tiled=True
        ).astype(jnp.float32),
        lax.psum_scatter(
            grad_bias_one.astype(jnp.bfloat16), "shard", scatter_dimension=0, tiled=True
        ).astype(jnp.float32),
        lax.psum_scatter(
            grad_qkv_weight.astype(jnp.bfloat16), "shard", scatter_dimension=0, tiled=True
        ).astype(jnp.float32),
        lax.psum_scatter(
            grad_qv_bias.astype(jnp.bfloat16), "shard", scatter_dimension=1, tiled=True
        ).astype(jnp.float32),
        lax.psum_scatter(
            grad_table_all.astype(jnp.bfloat16), "shard", scatter_dimension=1, tiled=True
        ).astype(jnp.float32),
        lax.psum_scatter(
            grad_proj_weight.astype(jnp.bfloat16), "shard", scatter_dimension=0, tiled=True
        ).astype(jnp.float32),
        lax.psum_scatter(
            grad_proj_bias.astype(jnp.bfloat16), "shard", scatter_dimension=0, tiled=True
        ).astype(jnp.float32),
    )
    summed = (
        lax.psum(attn_shares[0].astype(jnp.bfloat16), "seq").astype(jnp.float32),
        lax.psum(attn_shares[1].astype(jnp.bfloat16), "seq").astype(jnp.float32),
        lax.psum(attn_shares[2].astype(jnp.bfloat16), "seq").astype(jnp.float32),
        lax.psum(attn_shares[3].astype(jnp.bfloat16), "seq").astype(jnp.float32),
        lax.psum(attn_shares[4].astype(jnp.bfloat16), "seq").astype(jnp.float32),
        lax.psum(attn_shares[5].astype(jnp.bfloat16), "seq").astype(jnp.float32),
        lax.psum(attn_shares[6].astype(jnp.bfloat16), "seq").astype(jnp.float32),
        lax.psum(mlp_shares[0].astype(jnp.bfloat16), "seq").astype(jnp.float32),
        lax.psum(mlp_shares[1].astype(jnp.bfloat16), "seq").astype(jnp.float32),
        lax.psum(mlp_shares[2].astype(jnp.bfloat16), "seq").astype(jnp.float32),
        lax.psum(mlp_shares[3].astype(jnp.bfloat16), "seq").astype(jnp.float32),
        lax.psum(mlp_shares[4].astype(jnp.bfloat16), "seq").astype(jnp.float32),
        lax.psum(mlp_shares[5].astype(jnp.bfloat16), "seq").astype(jnp.float32),
    )
    return (
        result.reshape(images, local_rows, columns, D),
        grad_inputs.reshape(images, local_rows, columns, D),
        summed[0],
        summed[1],
        summed[2],
        summed[3],
        summed[4],
        summed[5],
        summed[6],
        summed[7],
        summed[8],
        summed[9],
        summed[10],
        summed[11],
        summed[12],
    )


def solution(mesh):
    return jax.shard_map(
        per_device,
        mesh=mesh,
        in_specs=(
            P("shard", "seq", None, None),
            P("shard", None, None),
            P("shard", "seq", None, None),
            P("shard"),
            P("shard"),
            P("shard", None),
            P(None, "shard"),
            P(None, "shard"),
            P("shard", None),
            P("shard"),
            P("shard"),
            P("shard"),
            P("shard", None),
            P("shard"),
            P("shard", None),
            P("shard"),
        ),
        out_specs=(
            P("shard", "seq", None, None),
            P("shard", "seq", None, None),
            P("shard"),
            P("shard"),
            P("shard", None),
            P(None, "shard"),
            P(None, "shard"),
            P("shard", None),
            P("shard"),
            P("shard"),
            P("shard"),
            P("shard", None),
            P("shard"),
            P("shard", None),
            P("shard"),
        ),
        check_vma=False,
    )
```

profile of v0, /device:TPU:0, one launch (start us, length us, event | category | flops | bytes accessed | tf_op | source)
XLA Modules:
  0.0 767.6 jit_solution(10089235293077118916)
XLA Ops:
  14.2 15.5 %all-reduce.15 = (bf16[512]{0:T(512)(128)(2,1)S(1)}, bf16[512]{0:T(512)(128)(2,1)S(1)}, bf16[512]{0:T(512)(128)(2,1)S(1)}, bf16[512]{0:T(512)(128)(2,1)S(1)}, bf16[512]{0:T(512)(128)(2,1)S(1)}) all-reduce(bf16[512]{0:T(512)(128)(2,1)S(1)} %dynamic-update-slice.1, ...), channel_id=1, replica_groups=mesh['shard'=8,'seq'=4] {'shard'}, use_global_device_ids=true, to_apply=%add.1 | all-reduce | flops 2560 | bytes 10240
  38.4 7.9 %all-gather = bf16[8,64,2]{1,2,0:T(2,128)(2,1)S(1)} all-gather(bf16[1,64,2]{1,2,0:T(2,128)(2,1)S(1)} %bitcast.196), channel_id=1, replica_groups=mesh['shard'=8,'seq'=4] {'shard'}, dimensions={0}, use_global_device_ids=true | all-gather | bytes 2304 | tf_op jit(solution)/shard_map/all_gather | solution.py:92
  69.1 8.7 %all-gather.1 = bf16[8,2,169]{2,1,0:T(2,128)(2,1)S(1)} all-gather(bf16[1,2,169]{2,1,0:T(2,128)(2,1)S(1)} %bitcast.195), channel_id=1, replica_groups=mesh['shard'=8,'seq'=4] {'shard'}, dimensions={0}, use_global_device_ids=true | all-gather | bytes 6084 | tf_op jit(solution)/shard_map/all_gather | solution.py:93
  81.1 49.8 %all-to-all-done = bf16[3,1,7,112,16,32]{3,5,2,1,0,4:T(8,128)(2,1)S(1)} async-done(((bf16[3,1,7,112,16,32]{3,5,2,1,0,4:T(8,128)(2,1)}), bf16[3,1,7,112,16,32]{3,5,2,1,0,4:T(8,128)(2,1)S(1)}, u32[]{:S(2)}, u32[]{:S(2)}) %all-to-all-start) | async-done | bytes 2408480 | tf_op jit(solution)/shard_map/all_to_all | solution.py:123
  131.0 8.8 %copy.209 = bf16[3,1,7,112,4,4,32]{6,5,3,2,4,1,0:T(4,128)(2,1)} copy(bf16[3,1,7,112,4,4,32]{3,6,2,0,5,4,1:T(8,128)(2,1)S(1)} %bitcast.160) | data formatting | bytes 4816896 | tf_op jit(solution)/shard_map/all_to_all | solution.py:123
  139.8 7.8 %fusion.34 = (bf16[1,1,4,7,112,4,32]{6,5,4,3,2,1,0:T(4,128)(2,1)}, bf16[1,1,4,7,112,4,32]{6,5,4,3,2,1,0:T(4,128)(2,1)S(1)}, bf16[1,1,4,7,112,4,32]{6,5,4,3,2,1,0:T(4,128)(2,1)S(1)}) fusion(bf16[3,1,4,7,112,4,32]{6,5,4,3,2,1,0:T(4,128)(2,1)} %bitcast.141), kind=kLoop, calls=%fused_computation.116 | loop fusion | bytes 4816896 | tf_op jit(solution)/shard_map/slice | solution.py:143
  150.1 6.0 copy.212
  160.6 6.0 copy.213
  185.4 18.3 %copy.221 = bf16[64,4,49,32]{3,0,2,1:T(8,128)(2,1)S(1)} copy(bf16[64,4,49,32]{2,3,1,0:T(8,128)(2,1)} %convolution_convert_fusion.4) | data formatting | bytes 1605632 | tf_op jit(solution)/shard_map/convert_element_type | solution.py:151
  212.4 25.4 %all_to_all.60 = bf16[1,28,112,4,32]{2,4,3,0,1:T(8,128)(2,1)S(1)} all-to-all(bf16[1,28,112,4,32]{2,4,3,0,1:T(8,128)(2,1)S(1)} %copy.223), channel_id=1, replica_groups=mesh['shard'=8,'seq'=4] {'seq'}, dimensions={1} | all-to-all | bytes 1605632 | tf_op jit(solution)/shard_map/all_to_all | solution.py:153
  238.4 8.7 %all-gather.2 = bf16[8,1,256]{2,1,0:T(2,128)(2,1)S(1)} all-gather(bf16[1,1,256]{2,1,0:T(2,128)(2,1)S(1)} %reshape.481), channel_id=1, replica_groups=mesh['shard'=8,'seq'=4] {'shard'}, dimensions={0}, use_global_device_ids=true | all-gather | bytes 4608 | tf_op jit(solution)/shard_map/all_gather | solution.py:101
  247.1 10.6 %all_gather.44 = bf16[512,512]{1,0:T(8,128)(2,1)} all-gather(bf16[64,512]{1,0:T(8,128)(2,1)S(1)} %copy-done.25), channel_id=1, replica_groups=mesh['shard'=8,'seq'=4] {'shard'}, dimensions={0}, use_global_device_ids=true | all-gather | bytes 589824 | tf_op jit(solution)/shard_map/all_gather | solution.py:94
  261.7 19.5 %multiply_convert_fusion.1 = (bf16[784,2048]{1,0:T(8,128)(2,1)}, f32[784,2048]{1,0:T(8,128)}, f32[784,2048]{1,0:T(8,128)}) fusion(f32[2048]{0:T(1024)S(1)} %bitcast.193, bf16[512,2048]{1,0:T(8,128)(2,1)} %all-gather.9.cloned.1.call-done, f32[784,512]{1,0:T(8,128)S(1)} %get-tuple-element.78, f32[512]{0:T(512)S(1)} %convert_element_type.222, ...), kind=kOutput, calls=%fused_computation.10 | convolution fusion | flops 1752145920 | bytes 19777664 | tf_op jit(solution)/shard_map/dot_general | solution.py:167
  281.2 8.2 %fusion.40 = (bf16[2048]{0:T(1024)(128)(2,1)}, bf16[784,2048]{1,0:T(8,128)(2,1)S(1)}) fusion(f32[784,2048]{1,0:T(8,128)} %get-tuple-element.58, bf16[784,512]{1,0:T(8,128)(2,1)S(1)} %bitcast.162, bf16[2048,512]{1,0:T(8,128)(2,1)} %all-gather.11.cloned.1.call-done, f32[784,2048]{1,0:T(8,128)} %get-tuple-element.79, f32[2048]{0:T(1024)S(1)} %bitcast.194), kind=kOutput, calls=%fused_computation.122 | convolution fusion | flops 1669855232 | bytes 18968576 | tf_op jit(solution)/shard_map/dot_general | solution.py:51
  300.2 8.6 %collective-permute-done.2 = bf16[1,3,112,512]{2,3,1,0:T(8,128)(2,1)S(1)} collective-permute-done((bf16[1,3,112,512]{2,3,1,0:T(8,128)(2,1)S(1)}, bf16[1,3,112,512]{2,3,1,0:T(8,128)(2,1)S(1)}, u32[]{:S(2)}, u32[]{:S(2)}) %collective-permute-start.2) | collective-permute-done | bytes 344096 | tf_op jit(solution)/shard_map/ppermute | solution.py:18
  309.0 28.4 %all_to_all.61 = bf16[1,7,112,16,32]{2,4,1,0,3:T(8,128)(2,1)} all-to-all(bf16[1,7,112,16,32]{2,4,1,0,3:T(8,128)(2,1)S(1)} %copy.228), channel_id=1, replica_groups=mesh['shard'=8,'seq'=4] {'seq'}, dimensions={3} | all-to-all | bytes 1605632 | tf_op jit(solution)/shard_map/all_to_all | solution.py:221
  345.3 6.1 copy.231
  351.4 7.0 multiply_reduce_fusion
  371.0 7.4 copy.235
  382.7 7.2 copy.239
  390.0 6.0 copy.240
  396.0 7.2 copy.243
  407.8 10.8 %pad_maximum_fusion = bf16[3,1,28,112,4,32]{5,4,3,2,1,0:T(4,128)(2,1)} fusion(bf16[1,1,28,112,4,32]{5,4,3,2,1,0:T(4,128)(2,1)S(1)} %bitcast.148, bf16[1,1,28,112,4,32]{5,4,3,2,1,0:T(4,128)(2,1)S(1)} %bitcast.146, bf16[1,1,28,112,4,32]{5,4,3,2,1,0:T(4,128)(2,1)S(1)} %bitcast.144), kind=kLoop, calls=%fused_computation | loop fusion | flops 2408448 | bytes 4816896 | tf_op jit(solution)/shard_map/stack | solution.py:252
  418.6 10.1 %copy.245 = bf16[3,1,28,112,4,32]{3,5,4,1,0,2:T(8,128)(2,1)S(1)} copy(bf16[3,1,28,112,4,32]{5,4,3,2,1,0:T(4,128)(2,1)} %pad_maximum_fusion) | data formatting | bytes 4816896 | tf_op jit(solution)/shard_map/stack | solution.py:252
  428.7 64.5 %all_to_all.62 = bf16[3,1,28,112,4,32]{3,5,4,1,0,2:T(8,128)(2,1)S(1)} all-to-all(bf16[3,1,28,112,4,32]{3,5,4,1,0,2:T(8,128)(2,1)S(1)} %copy.245), channel_id=1, replica_groups=mesh['shard'=8,'seq'=4] {'seq'}, dimensions={2} | all-to-all | bytes 4816896 | tf_op jit(solution)/shard_map/all_to_all | solution.py:259
  544.7 6.0 collective-permute-done.3
  554.4 16.9 %reduce-scatter.10.cloned.1.call-done = bf16[64,512]{1,0:T(8,128)(2,1)} async-done(((bf16[512,512]{1,0:T(8,128)(2,1)}), bf16[64,512]{1,0:T(8,128)(2,1)}) %reduce-scatter.10.cloned.1.call-update) | async-done | bytes 65552 | tf_op jit(solution)/shard_map/reduce_scatter | solution.py:304
  571.3 44.4 %reduce-scatter.12.cloned.1.call-done = bf16[64,2048]{1,0:T(8,128)(2,1)} async-done(((bf16[512,2048]{1,0:T(8,128)(2,1)}), bf16[64,2048]{1,0:T(8,128)(2,1)}) %reduce-scatter.12.cloned.1.call-update) | async-done | bytes 262160 | tf_op jit(solution)/shard_map/reduce_scatter | solution.py:194
  615.7 44.9 %reduce-scatter.14.cloned.1.call-done = bf16[256,512]{1,0:T(8,128)(2,1)} async-done(((bf16[2048,512]{1,0:T(8,128)(2,1)}), bf16[256,512]{1,0:T(8,128)(2,1)}) %reduce-scatter.14.cloned.1.call-update) | async-done | bytes 262160 | tf_op jit(solution)/shard_map/reduce_scatter | solution.py:200
  660.6 42.4 %reduce-scatter.8.cloned.1.call-done = bf16[64,1536]{1,0:T(8,128)(2,1)} async-done(((bf16[512,1536]{1,0:T(8,128)(2,1)}), bf16[64,1536]{1,0:T(8,128)(2,1)}) %reduce-scatter.8.cloned.1.call-update) | async-done | bytes 196624 | tf_op jit(solution)/shard_map/reduce_scatter | solution.py:295
  706.8 23.9 %all-reduce.14 = (bf16[512]{0:T(512)(128)(2,1)S(1)}, bf16[512]{0:T(512)(128)(2,1)S(1)}, bf16[512]{0:T(512)(128)(2,1)S(1)}, bf16[169,16]{0,1:T(8,128)(2,1)S(1)}, ...) all-reduce(bf16[512]{0:T(512)(128)(2,1)S(1)} %copy-done.47, ...), channel_id=1, replica_groups=mesh['shard'=8,'seq'=4] {'shard'}, use_global_device_ids=true, to_apply=%add.5 | all-reduce | flops 8336 | bytes 33344
  731.2 12.4 %all-reduce.16 = (bf16[64]{0:T(256)(128)(2,1)S(1)}, bf16[64]{0:T(256)(128)(2,1)S(1)}, bf16[2,64]{1,0:T(2,128)(2,1)S(1)}, bf16[169,2]{0,1:T(2,128)(2,1)S(1)}, bf1...) all-reduce(bf16[64]{0:T(256)(128)(2,1)S(1)} %dynamic-slice.8, ...), channel_id=1, replica_groups=mesh['shard'=8,'seq'=4] {'seq'}, use_global_device_ids=true, to_apply=%region_13.14 | all-reduce | flops 1106 | bytes 4424 | tf_op jit(solution)/shard_map/psum | solution.py:312
  (298 shorter events, 194.1 us)
Async XLA Ops:
  7.2 31.2 %copy-start.48 = (bf16[2,64]{1,0:T(2,128)(2,1)S(1)}, bf16[2,64]{1,0:T(2,128)(2,1)}, u32[]{:S(2)}) copy-start(bf16[2,64]{1,0:T(2,128)(2,1)} %param.22) | copy-start | bytes 772
  7.2 39.6 %all-gather.7.cloned.1.call-start = ((), (), s32[]{:S(2)}) async-start(), calls=%async_computation.9 | async-start | bytes 1769472 | tf_op jit(solution)/shard_map/all_gather | solution.py:91
  29.7 8.7 %copy-start.26 = (f32[512]{0:T(512)}, f32[512]{0:T(512)S(1)}, u32[]{:S(2)}) copy-start(f32[512]{0:T(512)S(1)} %convert_element_type.212) | copy-start | bytes 6148
  33.3 13.0 %copy-start.28 = (f32[7,112]{1,0:T(8,128)}, f32[7,112]{1,0:T(8,128)S(1)}, u32[]{:S(2)}) copy-start(f32[7,112]{1,0:T(8,128)S(1)} %get-tuple-element.70) | copy-start | bytes 9412
  34.9 11.6 %collective-permute-start = (bf16[1,3,112,512]{3,2,1,0:T(8,128)(2,1)S(1)}, bf16[1,3,112,512]{3,2,1,0:T(8,128)(2,1)S(1)}, u32[]{:S(2)}, u32[]{:S(2)}) collective-permute-start(bf16[1,3,112,512]{3,2,1,0:T(8,128)(2,1)S(1)} %slice.122), channel_id=1, source_target_pairs={{0,3},{1,0},{2,1},{3,2},{4,7},{5,4},{6,5},{7,6},{8,11},{9,8},{10,9... | collective-permute-start | bytes 1032200 | tf_op jit(solution)/shard_map/ppermute | solution.py:18
  64.2 14.5 %copy-start.35 = (s32[1,28,112]{2,0,1:T(1,128)S(1)}, s32[1,28,112]{2,0,1:T(1,128)}, u32[]{:S(2)}) copy-start(s32[1,28,112]{2,0,1:T(1,128)} %param.17) | copy-start | bytes 37636
  64.2 66.8 %all-to-all-start = ((bf16[3,1,7,112,16,32]{3,5,2,1,0,4:T(8,128)(2,1)}), bf16[3,1,7,112,16,32]{3,5,2,1,0,4:T(8,128)(2,1)S(1)}, u32[]{:S(2)}, u32[]{:S(2)}) async-start(bf16[3,1,7,112,16,32]{3,5,2,1,0,4:T(8,128)(2,1)} %copy.208), calls=%async_computation | async-start | bytes 5505024 | tf_op jit(solution)/shard_map/all_to_all | solution.py:123
  68.0 193.7 %all-gather.9.cloned.1.call-start = ((), (), s32[]{:S(2)}) async-start(), calls=%async_computation.10 | async-start | bytes 2359296 | tf_op jit(solution)/shard_map/all_gather | solution.py:100
  68.8 212.4 %all-gather.11.cloned.1.call-start = ((), (), s32[]{:S(2)}) async-start(), calls=%async_computation.11 | async-start | bytes 2359296 | tf_op jit(solution)/shard_map/all_gather | solution.py:102
  69.0 8.8 %copy-start.36 = (s32[2401]{0:T(1024)}, s32[2401]{0:T(1024)S(1)}, u32[]{:S(2)}) copy-start(s32[2401]{0:T(1024)S(1)} %reshape.458) | copy-start | bytes 28816
  174.1 8.2 %copy-start.3 = (bf16[64,4,49,32]{2,3,1,0:T(8,128)(2,1)}, bf16[64,4,49,32]{2,3,1,0:T(8,128)(2,1)S(1)}, u32[]{:S(2)}) copy-start(bf16[64,4,49,32]{2,3,1,0:T(8,128)(2,1)S(1)} %copy.220) | copy-start | bytes 2408452
  212.4 26.0 %copy-start.50 = (bf16[256]{0:T(256)(128)(2,1)S(1)}, bf16[256]{0:T(256)(128)(2,1)}, u32[]{:S(2)}) copy-start(bf16[256]{0:T(256)(128)(2,1)} %param.29) | copy-start | bytes 1540
  212.4 34.7 %copy-start.25 = (bf16[64,512]{1,0:T(8,128)(2,1)S(1)}, bf16[64,512]{1,0:T(8,128)(2,1)}, u32[]{:S(2)}) copy-start(bf16[64,512]{1,0:T(8,128)(2,1)} %param.24) | copy-start | bytes 196612
  238.0 19.8 %collective-permute-start.1 = (bf16[1,3,112,512]{2,3,1,0:T(8,128)(2,1)S(1)}, bf16[1,3,112,512]{2,3,1,0:T(8,128)(2,1)S(1)}, u32[]{:S(2)}, u32[]{:S(2)}) collective-permute-start(bf16[1,3,112,512]{2,3,1,0:T(8,128)(2,1)S(1)} %slice.133), channel_id=1, source_target_pairs={{0,1},{1,2},{2,3},{3,0},{4,5},{5,6},{6,7},{7,4},{8,9},{9,10},{10,1... | collective-permute-start | bytes 1032200 | tf_op jit(solution)/shard_map/ppermute | solution.py:18
  238.3 305.1 %reduce-scatter.16.cloned.1.call-start = ((), (), s32[]{:S(2)}) async-start(), calls=%async_computation.16 | async-start | bytes 147456
  259.2 21.9 %copy-start.19 = (bf16[1,7,112,512]{3,2,1,0:T(8,128)(2,1)}, bf16[1,7,112,512]{3,2,1,0:T(8,128)(2,1)S(1)}, u32[]{:S(2)}) copy-start(bf16[1,7,112,512]{3,2,1,0:T(8,128)(2,1)S(1)} %copy.225) | copy-start | bytes 2408452
  261.3 30.9 %copy-start.7 = (f32[784,512]{1,0:T(8,128)}, f32[784,512]{1,0:T(8,128)S(1)}, u32[]{:S(2)}) copy-start(f32[784,512]{1,0:T(8,128)S(1)} %get-tuple-element.78) | copy-start | bytes 4816900
  261.7 19.5 %copy-start.11 = (bf16[1,7,112,512]{3,2,1,0:T(8,128)(2,1)S(1)}, bf16[1,7,112,512]{3,2,1,0:T(8,128)(2,1)}, u32[]{:S(2)}) copy-start(bf16[1,7,112,512]{3,2,1,0:T(8,128)(2,1)} %param.18) | copy-start | bytes 2408452
  281.2 8.2 %copy-start.49 = (bf16[512,2048]{1,0:T(8,128)(2,1)S(1)}, bf16[512,2048]{1,0:T(8,128)(2,1)}, u32[]{:S(2)}) copy-start(bf16[512,2048]{1,0:T(8,128)(2,1)} %all-gather.9.cloned.1.call-done) | copy-start | bytes 6291460
  296.5 12.2 %collective-permute-start.2 = (bf16[1,3,112,512]{2,3,1,0:T(8,128)(2,1)S(1)}, bf16[1,3,112,512]{2,3,1,0:T(8,128)(2,1)S(1)}, u32[]{:S(2)}, u32[]{:S(2)}) collective-permute-start(bf16[1,3,112,512]{2,3,1,0:T(8,128)(2,1)S(1)} %pad_maximum_fusion.7), channel_id=1, source_target_pairs={{0,3},{1,0},{2,1},{3,2},{4,7},{5,4},{6,5},{7,6},{8,11},{9,8},{10,9... | collective-permute-start | bytes 1032200 | tf_op jit(solution)/shard_map/ppermute | solution.py:18
  345.3 13.1 %slice-start = ((s8[7340032]{0:T(1024)(128)(4,1)}), s8[3145728]{0:T(1024)(128)(4,1)S(1)}, s32[]{:S(2)}) async-start(s8[7340032]{0:T(1024)(128)(4,1)} %bitcast.139), calls=%async_computation.18 | async-start | bytes 6291456
  501.7 69.6 %reduce-scatter.10.cloned.1.call-start = ((), (), s32[]{:S(2)}) async-start(), calls=%async_computation.13 | async-start | bytes 589824 | tf_op jit(solution)/shard_map/reduce_scatter | solution.py:304
  504.4 111.3 %reduce-scatter.12.cloned.1.call-start = ((), (), s32[]{:S(2)}) async-start(), calls=%async_computation.14 | async-start | bytes 2359296 | tf_op jit(solution)/shard_map/reduce_scatter | solution.py:194
  510.4 150.2 %reduce-scatter.14.cloned.1.call-start = ((), (), s32[]{:S(2)}) async-start(), calls=%async_computation.15 | async-start | bytes 2359296 | tf_op jit(solution)/shard_map/reduce_scatter | solution.py:200
  516.2 186.8 %reduce-scatter.8.cloned.1.call-start = ((), (), s32[]{:S(2)}) async-start(), calls=%async_computation.12 | async-start | bytes 1769472 | tf_op jit(solution)/shard_map/reduce_scatter | solution.py:295
  531.0 222.9 %all-reduce.20.cloned.1.call-start = ((), (), s32[]{:S(2)}) async-start(), calls=%async_computation.17 | async-start | bytes 1572864 | tf_op jit(solution)/shard_map/psum | solution.py:314
  540.1 10.6 %copy-start.2 = (bf16[1,7,112,512]{3,2,1,0:T(8,128)(2,1)S(1)}, bf16[1,7,112,512]{3,2,1,0:T(8,128)(2,1)}, u32[]{:S(2)}) copy-start(bf16[1,7,112,512]{3,2,1,0:T(8,128)(2,1)} %param.16) | copy-start | bytes 2408452
  540.2 10.4 %collective-permute-start.3 = (bf16[1,3,112,512]{3,2,1,0:T(8,128)(2,1)S(1)}, bf16[1,3,112,512]{3,2,1,0:T(8,128)(2,1)S(1)}, u32[]{:S(2)}, u32[]{:S(2)}) collective-permute-start(bf16[1,3,112,512]{3,2,1,0:T(8,128)(2,1)S(1)} %pad_maximum_fusion.8), channel_id=1, source_target_pairs={{0,1},{1,2},{2,3},{3,0},{4,5},{5,6},{6,7},{7,4},{8,9},{9,10},{10,1... | collective-permute-start | bytes 1032200 | tf_op jit(solution)/shard_map/ppermute | solution.py:18
  550.7 152.3 %copy-start.27 = (f32[512]{0:T(512)S(1)}, f32[512]{0:T(512)}, u32[]{:S(2)}) copy-start(f32[512]{0:T(512)} %copy-done.26) | copy-start | bytes 6148
  550.7 152.3 %copy-start.31 = (f32[784]{0:T(1024)S(1)}, f32[784]{0:T(1024)}, u32[]{:S(2)}) copy-start(f32[784]{0:T(1024)} %copy-done.30) | copy-start | bytes 9412
  550.7 152.3 %copy-start.34 = (f32[784]{0:T(1024)S(1)}, f32[784]{0:T(1024)}, u32[]{:S(2)}) copy-start(f32[784]{0:T(1024)} %div.69) | copy-start | bytes 9412
  703.1 28.1 %copy-start.42 = (bf16[2,64]{1,0:T(2,128)(2,1)S(1)}, bf16[2,64]{1,0:T(2,128)(2,1)}, u32[]{:S(2)}) copy-start(bf16[2,64]{1,0:T(2,128)(2,1)} %copy.253) | copy-start | bytes 772
  (36 other events, 133.2 us)
Sparse Core Ops, SparseCore 0:
  9.9 28.5 all-gather.6
  70.7 28.3 all-gather.8
  238.4 28.6 all-gather.10
  501.8 31.4 reduce-scatter.15
  537.1 34.1 reduce-scatter.9
  574.4 41.2 reduce-scatter.11
  619.3 41.2 reduce-scatter.13
  664.5 38.4 reduce-scatter.7
  705.6 44.9 all-reduce.19
where the time goes:
time: 778 us; the launch traced here: 768 us
  waiting for transfers between devices  215 us (28%)
  blocking collectives  206 us (26%)
  local copies, waits for them, and re-layouts  174 us (22%)
  matrix products  89.7 us (12%)
  other arithmetic  53.5 us (7%)
  between operations  18 us (2%)
  starting transfers between devices  11.6 us (1%)
    all_to_all x1, blocking collectives, per_device(): lax.all_to_all(grad_stacked, 'seq', split_axis=2, concat_axis=4, tiled=True)  64.5 us
    all_to_all x1, waiting for transfers between devices, per_device(): lax.all_to_all(stacked, 'seq', split_axis=4, concat_axis=2, tiled=True)  49.8 us
    reduce_scatter x1, waiting for transfers between devices, per_device(): lax.psum_scatter(grad_out_weight.astype(jnp.bfloat16), 'shard', scatter_d...  44.9 us
    reduce_scatter x1, waiting for transfers between devices, per_device(): lax.psum_scatter(grad_in_weight.astype(jnp.bfloat16), 'shard', scatter_di...  44.4 us
    reduce_scatter x1, waiting for transfers between devices, per_device(): lax.psum_scatter(grad_qkv_weight.astype(jnp.bfloat16), 'shard', scatter_d...  42.4 us
    unnamed x2, blocking collectives  39.4 us
    all_to_all x1, blocking collectives, per_device(): lax.all_to_all(grad_attended, 'seq', split_axis=3, concat_axis=1, tiled=T...  28.4 us
    all_to_all x1, blocking collectives, per_device(): lax.all_to_all(attended_tok, 'seq', split_axis=1, concat_axis=3, tiled=True)  25.4 us
  transfers between devices with their start and end apart: 14, of which 7 were waited for; matrix products, arithmetic and copies ran while one was open for 23% of the time, Pallas kernels for 0%

commit v1 on v0

v1 whole, which is shorter than its diff:
```python
import jax
import jax.numpy as jnp
from jax import lax
from jax.experimental import pallas as pl
from jax.experimental.pallas import tpu as pltpu
from jax.sharding import PartitionSpec as P

D = 512
HEADS = 16
HEAD = 32
WIN = 7
SHIFT = 3
FF = 2048
WIDTH = 112
WINDOWS = WIDTH // WIN
SLOT = 8
PLACES = WIN * SLOT
GROUP = 8
GROUPS = HEADS // GROUP
FEAT = GROUP * HEAD
LANES = 64 * GROUP
TOKENS = WIN * WIDTH
PADDED = WINDOWS * PLACES
TAB = 1536
TAB_USED = 768
SMALL = 16
EPS = 1e-05
SCALE = HEAD**-0.5
BF = jnp.bfloat16
F32 = jnp.float32
VMEM_LIMIT = 60 * 1024 * 1024


def shifted_2(value, axis, by):
    peers = lax.axis_size(axis)
    return lax.ppermute(value, axis, [(i, (i + by) % peers) for i in range(peers)])


def dot(left, right, dims=((1,), (0,))):
    return lax.dot_general(left, right, (dims, ((), ())), preferred_element_type=F32)


def dot_nt(left, right):
    return dot(left, right, ((1,), (1,)))


def dot_tn(left, right):
    return dot(left, right, ((0,), (0,)))


def iota(shape, axis):
    return lax.broadcasted_iota(jnp.int32, shape, axis)


def one_hot(condition):
    return jnp.where(condition, 1.0, 0.0).astype(BF)


def column_places():
    slot = iota((WINDOWS * SLOT, WIDTH), 0)
    column = iota((WINDOWS * SLOT, WIDTH), 1)
    place = slot & (SLOT - 1)
    wanted = (slot >> 3) * WIN + place + SHIFT
    wanted = jnp.where(wanted >= WIDTH, wanted - WIDTH, wanted)
    return one_hot((wanted == column) & (place < WIN))


def places_column():
    slot = iota((WIDTH, WINDOWS * SLOT), 1)
    column = iota((WIDTH, WINDOWS * SLOT), 0)
    place = slot & (SLOT - 1)
    wanted = (slot >> 3) * WIN + place + SHIFT
    wanted = jnp.where(wanted >= WIDTH, wanted - WIDTH, wanted)
    return one_hot((wanted == column) & (place < WIN))


def spread_matrix():
    return one_hot((iota((LANES, PLACES), 0) >> 3) == iota((LANES, PLACES), 1))


def fold_matrix():
    return one_hot((iota((PLACES, LANES), 1) >> 3) == iota((PLACES, LANES), 0))


def head_mask(value):
    row = iota((LANES, FEAT), 0) & (GROUP - 1)
    feature = iota((LANES, FEAT), 1) >> 5
    return jnp.where(row == feature, value, 0.0).astype(F32)


def table_pick(row_axis, backwards):
    shape = (TAB_USED, LANES) if row_axis == 0 else (LANES, TAB_USED)
    lane = iota(shape, row_axis)
    pair = iota(shape, 1 - row_axis)
    place = pair >> 3
    row, column = place >> 3, place & (SLOT - 1)
    entry = row * (2 * WIN - 1) + column
    if backwards:
        entry = (WIN - 1) * 2 * WIN - entry
    match = ((lane >> 3) == entry) & ((lane & 7) == (pair & 7))
    return one_hot(match & (column < WIN) & (row < WIN))


def norm_stats(values):
    average = jnp.mean(values, -1, keepdims=True)
    centered = values - average
    variance = jnp.mean(centered * centered, -1, keepdims=True)
    scale = lax.rsqrt(variance + EPS)
    return centered * scale, scale


def norm_back(grad, normed, scale, gain):
    scaled = grad * gain
    first = jnp.mean(scaled, -1, keepdims=True)
    second = jnp.mean(scaled * normed, -1, keepdims=True)
    return scale * (scaled - first - normed * second)


def whole(memory=pltpu.VMEM):
    return pl.BlockSpec(memory_space=memory)


def kernel_call(body, outs, ins, scratch=(), flops=0, smem=0):
    size = sum(a.size * a.dtype.itemsize for a in list(ins) + list(outs))
    return pl.pallas_call(
        body,
        out_shape=tuple(outs),
        in_specs=[whole(pltpu.SMEM)] * smem + [whole()] * (len(ins) - smem),
        out_specs=tuple(whole() for _ in outs),
        scratch_shapes=list(scratch),
        cost_estimate=pl.CostEstimate(flops=flops, bytes_accessed=size, transcendentals=0),
        compiler_params=pltpu.CompilerParams(vmem_limit_bytes=VMEM_LIMIT),
    )(*ins)


def like(shape, dtype):
    return jax.ShapeDtypeStruct(shape, dtype)


def pack_body(
    me_ref, g1, b1, wqkv, bqv, table, wproj, bproj, g2, b2, win, bin_, wout, bout, attn, mlp
):
    depth = wqkv.shape[0]
    me = me_ref[0]

    def place(vector, lanes):
        w = vector.shape[1]
        pick = one_hot(iota((w, lanes), 1) == iota((w, lanes), 0) + me * w)
        wide = jnp.broadcast_to(vector, (8, w))
        return dot(wide.astype(BF), pick)[0:1]

    for c in range(3):
        attn[c * depth : (c + 1) * depth, :] = wqkv[:, c * D : (c + 1) * D]
    attn[3 * depth : 4 * depth, :] = wproj[...]
    rows = [
        place(g1[...], D),
        place(b1[...], D),
        place(bqv[0:1, :], D),
        place(bqv[1:2, :], D),
        place(bproj[...], D),
    ]
    entries, held = table.shape
    lane = iota((entries, TAB), 1)
    entry = iota((entries, TAB), 0)
    spot = entry * GROUP + TAB - (WIN - 1) * 2 * WIN * GROUP
    spot = jnp.where(spot >= TAB, spot - TAB, spot)
    values = table[...].astype(F32)
    groups = [jnp.zeros((1, TAB), F32) for _ in range(GROUPS)]
    for h in range(held):
        head = me * held + h
        inside = lane == spot + (head & (GROUP - 1))
        row = jnp.sum(jnp.where(inside, values[:, h : h + 1], 0.0), 0, keepdims=True)
        for g in range(GROUPS):
            groups[g] = groups[g] + jnp.where((head >> 3) == g, row, 0.0)
    for g in range(GROUPS):
        rows += [groups[g][:, c * D : (c + 1) * D] for c in range(TAB // D)]
    rows += [jnp.zeros((SMALL - len(rows), D), F32)]
    attn[4 * depth :, :] = jnp.concatenate(rows, 0).astype(BF)

    for c in range(FF // D):
        mlp[c * depth : (c + 1) * depth, :] = win[:, c * D : (c + 1) * D]
    mlp[4 * depth : 8 * depth, :] = wout[...]
    hidden_bias = place(bin_[...], FF)
    rows = [place(g2[...], D), place(b2[...], D), place(bout[...], D)]
    rows += [hidden_bias[:, c * D : (c + 1) * D] for c in range(FF // D)]
    rows += [jnp.zeros((SMALL - len(rows), D), F32)]
    mlp[8 * depth :, :] = jnp.concatenate(rows, 0).astype(BF)


def unpack_body(
    me_ref, attn, mlp, g1, b1, wqkv, bqv, table, wproj, bproj, g2, b2, win, bin_, wout, bout
):
    depth = wqkv.shape[0]
    me = me_ref[0]

    def mine(row, w):
        lanes = row.shape[1]
        pick = one_hot(iota((lanes, w), 0) == iota((lanes, w), 1) + me * w)
        wide = jnp.broadcast_to(row, (8, lanes))
        return dot(wide.astype(BF), pick)[0:1]

    for c in range(3):
        wqkv[:, c * D : (c + 1) * D] = attn[c * depth : (c + 1) * depth, :].astype(F32)
    wproj[...] = attn[3 * depth : 4 * depth, :].astype(F32)
    small = attn[4 * depth :, :].astype(F32)
    w = D * depth // D
    g1[...] = mine(small[0:1], w)
    b1[...] = mine(small[1:2], w)
    bqv[0:1, :] = mine(small[2:3], w)
    bqv[1:2, :] = mine(small[3:4], w)
    bproj[...] = mine(small[4:5], w)
    entries, held = table.shape
    lane = iota((entries, TAB), 1)
    spot = (entries - 1 - iota((entries, TAB), 0)) * GROUP
    parts = TAB // D
    rows = [
        jnp.concatenate([small[5 + g * parts + c : 6 + g * parts + c] for c in range(parts)], 1)
        for g in range(GROUPS)
    ]
    which = iota((entries, held), 1)
    total = jnp.zeros((entries, held), F32)
    for h in range(held):
        head = me * held + h
        row = rows[0]
        for g in range(1, GROUPS):
            row = jnp.where((head >> 3) == g, rows[g], row)
        inside = lane == spot + (head & (GROUP - 1))
        column = jnp.sum(jnp.where(inside, row, 0.0), 1, keepdims=True)
        total = jnp.where(which == h, column, total)
    table[...] = total

    for c in range(FF // D):
        win[:, c * D : (c + 1) * D] = mlp[c * depth : (c + 1) * depth, :].astype(F32)
    wout[...] = mlp[4 * depth : 8 * depth, :].astype(F32)
    small = mlp[8 * depth :, :].astype(F32)
    g2[...] = mine(small[0:1], w)
    b2[...] = mine(small[1:2], w)
    bout[...] = mine(small[2:3], w)
    bin_[...] = mine(
        jnp.concatenate([small[3 + c : 4 + c] for c in range(FF // D)], 1), w * FF // D
    )


def block_of(slab, c, depth):
    return slab[:, c * depth : (c + 1) * depth, :].reshape(D, D)


def smalls_of(slab, start):
    return jnp.sum(slab[:, start:, :].astype(F32), 0)


def attn_forward_body(
    tokens,
    halo,
    slab,
    reg_rows,
    reg_lanes,
    mixed,
    normed_win,
    query,
    key,
    value,
    probs,
    restored,
    wide,
    spread,
    fold,
    mask,
    bias,
):
    depth = (slab.shape[1] - SMALL) // 4
    small = smalls_of(slab, 4 * depth)
    gain, offset = small[0:1], small[1:2]
    bias_q, bias_v, bias_o = small[2:3], small[3:4], small[4:5]
    spread[...] = spread_matrix()
    fold[...] = fold_matrix()
    mask[...] = head_mask(1.0)
    pick = table_pick(0, False)
    parts = TAB // D
    empty = (iota((PLACES, LANES), 0) & (SLOT - 1)) == WIN
    for g in range(GROUPS):
        row = jnp.concatenate([small[5 + g * parts + c : 6 + g * parts + c] for c in range(parts)], 1)
        row = jnp.broadcast_to(row, (SLOT, TAB))
        row = pltpu.roll(row, 0, 1, stride=GROUP, stride_axis=0)
        turned = [
            pltpu.roll(row, (2 * WIN - 1) * GROUP * r, 1)[:, :TAB_USED] for r in range(WIN)
        ]
        picked = dot(jnp.concatenate(turned, 0).astype(BF), pick)
        bias[g] = jnp.where(empty, -1e30, picked)

    columns = column_places()
    own = WIN - SHIFT
    for r in range(WIN):
        x = (tokens[SHIFT + r] if r < own else halo[r - own]).astype(F32)
        normed, _ = norm_stats(x)
        low = (normed * gain + offset).astype(BF)
        wide[:, r] = dot(columns, low).reshape(WINDOWS, SLOT, D)
    normed_win[...] = wide[...].reshape(PADDED, D).astype(BF)
    query[...] = (dot(normed_win[...], block_of(slab, 0, depth)) + bias_q).astype(BF)
    key[...] = dot(normed_win[...], block_of(slab, 1, depth)).astype(BF)
    value[...] = (dot(normed_win[...], block_of(slab, 2, depth)) + bias_v).astype(BF)

    def pair(n, carry):
        rows = pl.ds(pl.multiple_of(n * 2 * PLACES, 2 * PLACES), 2 * PLACES)
        for g in range(GROUPS):
            feats = slice(g * FEAT, (g + 1) * FEAT)
            q2 = query[rows, feats].astype(F32)
            k2 = key[rows, feats].astype(F32)
            v2 = value[rows, feats].astype(F32)
            held = []
            for s in range(2):
                w = 2 * n + s
                part = slice(s * PLACES, (s + 1) * PLACES)
                q, k, v = (a[part].astype(BF) for a in (q2, k2, v2))
                q_big = (dot(spread[...], q) * mask[...]).astype(BF)
                penalty = jnp.where(reg_rows[w][:, 0:1] != reg_lanes[w], -100.0, 0.0)
                logits = dot_nt(k, q_big) * SCALE + bias[g] + penalty
                top = jnp.max(logits, 0, keepdims=True)
                powers = jnp.exp(logits - top)
                p = powers * (1.0 / jnp.sum(powers, 0, keepdims=True))
                held.append(p)
                o_big = (dot_tn(p.astype(BF), v) * mask[...]).astype(BF)
                o = dot(fold[...], o_big)
                wide[w, :, :, feats] = o.reshape(WIN, SLOT, FEAT)
            probs[n, g] = jnp.concatenate(held, 0).astype(BF)
        return carry

    lax.fori_loop(0, WINDOWS // 2, pair, 0)
    back = places_column()
    for r in range(WIN):
        here = wide[:, r].reshape(WINDOWS * SLOT, D).astype(BF)
        restored[r * WIDTH : (r + 1) * WIDTH, :] = dot(back, here).astype(BF)
    branch = dot(restored[...], block_of(slab, 3, depth)) + bias_o
    for r in range(WIN):
        x = (tokens[SHIFT + r] if r < own else halo[r - own]).astype(F32)
        part = slice(r * WIDTH, (r + 1) * WIDTH)
        mixed[part, :] = x + branch[part]


def gelu_parts(h):
    size = jnp.abs(h) * (0.5**0.5)
    t = 1.0 / (1.0 + 0.3275911 * size)
    bell = jnp.exp(-0.5 * h * h)
    poly = t * (
        0.254829592
        + t * (-0.284496736 + t * (1.421413741 + t * (-1.453152027 + t * 1.061405429)))
    )
    tail = 0.5 * poly * bell
    upto = jnp.where(h >= 0, 1.0 - tail, tail)
    return upto, bell * 0.3989422804014327


def mlp_body(
    mixed, cotangent, halo, slab, kept, sent, grad_mixed, grads, normed_low, cot, out_sum, back_sum
):
    shards, height = slab.shape[:2]
    depth = (height - SMALL) // 8
    span = shards * D // FF
    small = smalls_of(slab, 8 * depth)
    gain, offset, bias_o = small[0:1], small[1:2], small[2:3]
    own = WIN - SHIFT
    for r in range(WIN):
        part = slice(r * WIDTH, (r + 1) * WIDTH)
        cot[part, :] = cotangent[SHIFT + r] if r < own else halo[r - own]
    normed, _ = norm_stats(mixed[...])
    normed_low[...] = (normed * gain + offset).astype(BF)
    vectors = []
    for c in range(FF // D):
        w_in = block_of(slab, c, depth)
        w_out = slab[c * span : (c + 1) * span, 4 * depth : 8 * depth, :].reshape(D, D)
        hidden = dot(normed_low[...], w_in) + small[3 + c : 4 + c]
        upto, density = gelu_parts(hidden)
        active = (hidden * upto).astype(BF)
        slope = upto + hidden * density
        grad = (dot_nt(cot[...], w_out) * slope).astype(BF)
        forward = dot(active, w_out)
        backward = dot_nt(grad, w_in)
        if c == 0:
            out_sum[...] = forward
            back_sum[...] = backward
        else:
            out_sum[...] += forward
            back_sum[...] += backward
        vectors.append(jnp.sum(grad.astype(F32), 0, keepdims=True))
        grads[:, c * depth : (c + 1) * depth, :] = (
            dot_tn(normed_low[...], grad).astype(BF).reshape(shards, depth, D)
        )
        grads[c * span : (c + 1) * span, 4 * depth : 8 * depth, :] = (
            dot_tn(active, cot[...]).astype(BF).reshape(span, 4 * depth, D)
        )
    result = mixed[...] + out_sum[...] + bias_o
    kept[...] = result[: own * WIDTH]
    sent[...] = result[own * WIDTH :].astype(BF)
    normed, scale = norm_stats(mixed[...])
    g = back_sum[...]
    rows = [
        jnp.sum(g * normed, 0, keepdims=True),
        jnp.sum(g, 0, keepdims=True),
        jnp.sum(cot[...].astype(F32), 0, keepdims=True),
    ] + vectors
    rows += [jnp.zeros((SMALL - len(rows), D), F32)]
    grads[:, 8 * depth :, :] = jnp.broadcast_to(
        jnp.concatenate(rows, 0).astype(BF)[None], (shards, SMALL, D)
    )
    grad_mixed[...] = cot[...].astype(F32) + norm_back(g, normed, scale, gain)


def attn_backward_body(
    grad_mixed,
    tokens,
    halo,
    slab,
    normed_win,
    query,
    key,
    value,
    probs,
    restored,
    kept,
    sent,
    grads,
    wide,
    grad_qkv,
    spread,
    fold,
    mask,
    pairs,
):
    shards = slab.shape[0]
    depth = (slab.shape[1] - SMALL) // 4
    small = smalls_of(slab, 4 * depth)
    gain = small[0:1]
    spread[...] = spread_matrix()
    fold[...] = fold_matrix()
    mask[...] = head_mask(1.0)
    pairs[...] = jnp.zeros_like(pairs)
    own = WIN - SHIFT

    def store(c, grad):
        grads[:, c * depth : (c + 1) * depth, :] = grad.astype(BF).reshape(shards, depth, D)

    branch = grad_mixed[...].astype(BF)
    bias_o = jnp.sum(branch.astype(F32), 0, keepdims=True)
    store(3, dot_tn(restored[...], branch))
    grad_att = dot_nt(branch, block_of(slab, 3, depth)).astype(BF)
    columns = column_places()
    for r in range(WIN):
        wide[:, r] = dot(columns, grad_att[r * WIDTH : (r + 1) * WIDTH]).reshape(WINDOWS, SLOT, D)

    def pair(n, carry):
        rows = pl.ds(pl.multiple_of(n * 2 * PLACES, 2 * PLACES), 2 * PLACES)
        for g in range(GROUPS):
            feats = slice(g * FEAT, (g + 1) * FEAT)
            q2 = query[rows, feats].astype(F32)
            k2 = key[rows, feats].astype(F32)
            v2 = value[rows, feats].astype(F32)
            p2 = probs[n, g].astype(F32)
            held = []
            for s in range(2):
                w = 2 * n + s
                part = slice(s * PLACES, (s + 1) * PLACES)
                q, k, v, p_low = (a[part].astype(BF) for a in (q2, k2, v2, p2))
                p = p2[part]
                go = wide[w, :, :, feats].reshape(PLACES, FEAT).astype(BF)
                go_big = (dot(spread[...], go) * mask[...]).astype(BF)
                q_big = (dot(spread[...], q) * mask[...]).astype(BF)
                dp = dot_nt(v, go_big)
                dv = dot(p_low, go_big)
                inner = jnp.sum(p * dp, 0, keepdims=True)
                ds = (p * (dp - inner)).astype(BF)
                pairs[g] += ds.astype(F32)
                dk = dot(ds, q_big) * SCALE
                dq_big = (dot_tn(ds, k) * (mask[...] * SCALE)).astype(BF)
                dq = dot(fold[...], dq_big)
                held.append((dq, dk, dv))
            for c in range(3):
                both = jnp.concatenate([held[0][c], held[1][c]], 0).astype(BF)
                grad_qkv[rows, c * D + g * FEAT : c * D + (g + 1) * FEAT] = both
        return carry

    lax.fori_loop(0, WINDOWS // 2, pair, 0)
    vectors = []
    for c in range(3):
        g = grad_qkv[:, c * D : (c + 1) * D]
        if c != 1:
            vectors.append(jnp.sum(g.astype(F32), 0, keepdims=True))
        store(c, dot_tn(normed_win[...], g))
        part = dot_nt(g, block_of(slab, c, depth))
        total = part if c == 0 else total + part
    wide[...] = total.reshape(WINDOWS, WIN, SLOT, D)
    back = places_column()
    gain_sum = jnp.zeros((1, D), F32)
    bias_sum = jnp.zeros((1, D), F32)
    for r in range(WIN):
        here = wide[:, r].reshape(WINDOWS * SLOT, D).astype(BF)
        g = dot(back, here)
        x = (tokens[SHIFT + r] if r < own else halo[r - own]).astype(F32)
        normed, scale = norm_stats(x)
        gain_sum += jnp.sum(g * normed, 0, keepdims=True)
        bias_sum += jnp.sum(g, 0, keepdims=True)
        grad = grad_mixed[r * WIDTH : (r + 1) * WIDTH, :] + norm_back(g, normed, scale, gain)
        if r < own:
            kept[r * WIDTH : (r + 1) * WIDTH, :] = grad
        else:
            sent[(r - own) * WIDTH : (r - own + 1) * WIDTH, :] = grad.astype(BF)

    pick = table_pick(1, True)
    rows = [gain_sum, bias_sum, vectors[0], vectors[1], bias_o]
    for g in range(GROUPS):
        high = pairs[g].astype(BF)
        low = (pairs[g] - high.astype(F32)).astype(BF)
        laid = dot(high, pick) + dot(low, pick)
        laid = jnp.concatenate([laid, jnp.zeros((PLACES, TAB - TAB_USED), F32)], 1)
        total = jnp.zeros((SLOT, TAB), F32)
        for r in range(WIN):
            total += pltpu.roll(
                laid[r * SLOT : (r + 1) * SLOT], (2 * WIN - 1) * GROUP * r, 1
            )
        total = pltpu.roll(total, 0, 1, stride=GROUP, stride_axis=0)
        row = jnp.sum(total, 0, keepdims=True)
        rows += [row[:, c * D : (c + 1) * D] for c in range(TAB // D)]
    rows += [jnp.zeros((SMALL - len(rows), D), F32)]
    grads[:, 4 * depth :, :] = jnp.broadcast_to(
        jnp.concatenate(rows, 0).astype(BF)[None], (shards, SMALL, D)
    )


def region_views(regions, rows, place):
    here = lax.dynamic_slice_in_dim(regions[0], place * rows, rows, 0)
    windows = here.reshape(WIN, WINDOWS, WIN).transpose(1, 0, 2)
    windows = jnp.pad(windows, ((0, 0), (0, 0), (0, SLOT - WIN))).astype(F32)
    windows = windows.reshape(WINDOWS, PLACES)
    by_row = jnp.broadcast_to(windows[:, :, None], (WINDOWS, PLACES, 128))
    by_lane = jnp.pad(jnp.repeat(windows, GROUP, 1), ((0, 0), (0, LANES - PLACES * GROUP)))
    return by_row, by_lane[:, None, :]


def per_device(
    tokens,
    regions,
    cotangent,
    gain_one,
    bias_one,
    w_qkv,
    bias_qv,
    table,
    w_proj,
    bias_proj,
    gain_two,
    bias_two,
    w_in,
    bias_in,
    w_out,
    bias_out,
):
    images, local_rows, columns, _ = tokens.shape
    assert images == 1 and local_rows == WIN and columns == WIDTH
    shards = lax.axis_size("shard")
    me = lax.axis_index("shard").astype(jnp.int32).reshape(1)
    depth = D // shards
    own = WIN - SHIFT
    params = (
        gain_one[None],
        bias_one[None],
        w_qkv,
        bias_qv,
        table,
        w_proj,
        bias_proj[None],
        gain_two[None],
        bias_two[None],
        w_in,
        bias_in[None],
        w_out,
        bias_out[None],
    )
    attn_slab, mlp_slab = kernel_call(
        pack_body,
        [like((4 * depth + SMALL, D), BF), like((8 * depth + SMALL, D), BF)],
        (me,) + params,
        smem=1,
    )
    attn_all = lax.all_gather(attn_slab, "shard")
    mlp_all = lax.all_gather(mlp_slab, "shard")
    tokens_here = tokens[0]
    token_halo = shifted_2(tokens_here[:SHIFT], "seq", -1)
    cot_here = cotangent[0]
    cot_halo = shifted_2(cot_here[:SHIFT], "seq", -1)
    by_row, by_lane = region_views(regions, local_rows, lax.axis_index("seq"))

    mixed, normed_win, query, key, value, probs, restored = kernel_call(
        attn_forward_body,
        [
            like((TOKENS, D), F32),
            like((PADDED, D), BF),
            like((PADDED, D), BF),
            like((PADDED, D), BF),
            like((PADDED, D), BF),
            like((WINDOWS // 2, GROUPS, 2 * PLACES, LANES), BF),
            like((TOKENS, D), BF),
        ],
        (tokens_here, token_halo, attn_all, by_row, by_lane),
        scratch=[
            pltpu.VMEM((WINDOWS, WIN, SLOT, D), F32),
            pltpu.VMEM((LANES, PLACES), BF),
            pltpu.VMEM((PLACES, LANES), BF),
            pltpu.VMEM((LANES, FEAT), F32),
            pltpu.VMEM((GROUPS, PLACES, LANES), F32),
        ],
        flops=5_000_000_000,
    )
    out_kept, out_sent, grad_mixed, mlp_grads = kernel_call(
        mlp_body,
        [
            like((own * WIDTH, D), F32),
            like((SHIFT * WIDTH, D), BF),
            like((TOKENS, D), F32),
            like(mlp_all.shape, BF),
        ],
        (mixed, cot_here, cot_halo, mlp_all),
        scratch=[
            pltpu.VMEM((TOKENS, D), BF),
            pltpu.VMEM((TOKENS, D), BF),
            pltpu.VMEM((TOKENS, D), F32),
            pltpu.VMEM((TOKENS, D), F32),
        ],
        flops=10_000_000_000,
    )
    mlp_share = lax.psum_scatter(mlp_grads, "shard", scatter_dimension=0)
    out_halo = shifted_2(out_sent, "seq", 1)
    tok_kept, tok_sent, attn_grads = kernel_call(
        attn_backward_body,
        [
            like((own * WIDTH, D), F32),
            like((SHIFT * WIDTH, D), BF),
            like(attn_all.shape, BF),
        ],
        (
            grad_mixed,
            tokens_here,
            token_halo,
            attn_all,
            normed_win,
            query,
            key,
            value,
            probs,
            restored,
        ),
        scratch=[
            pltpu.VMEM((WINDOWS, WIN, SLOT, D), F32),
            pltpu.VMEM((PADDED, 3 * D), BF),
            pltpu.VMEM((LANES, PLACES), BF),
            pltpu.VMEM((PLACES, LANES), BF),
            pltpu.VMEM((LANES, FEAT), F32),
            pltpu.VMEM((GROUPS, PLACES, LANES), F32),
        ],
        flops=10_000_000_000,
    )
    attn_share = lax.psum_scatter(attn_grads, "shard", scatter_dimension=0)
    tok_halo = shifted_2(tok_sent, "seq", 1)
    attn_total, mlp_total = lax.psum((attn_share, mlp_share), "seq")
    shapes = [like(p.shape, F32) for p in params]
    summed = kernel_call(unpack_body, shapes, (me, attn_total, mlp_total), smem=1)

    def joined(halo, kept):
        return jnp.concatenate([halo.astype(F32), kept], 0).reshape(tokens.shape)

    grads = [s.reshape(p.shape) for s, p in zip(
        summed,
        (
            gain_one,
            bias_one,
            w_qkv,
            bias_qv,
            table,
            w_proj,
            bias_proj,
            gain_two,
            bias_two,
            w_in,
            bias_in,
            w_out,
            bias_out,
        ),
    )]
    return (joined(out_halo, out_kept), joined(tok_halo, tok_kept), *grads)


def solution(mesh):
    return jax.shard_map(
        per_device,
        mesh=mesh,
        in_specs=(
            P("shard", "seq", None, None),
            P("shard", None, None),
            P("shard", "seq", None, None),
            P("shard"),
            P("shard"),
            P("shard", None),
            P(None, "shard"),
            P(None, "shard"),
            P("shard", None),
            P("shard"),
            P("shard"),
            P("shard"),
            P("shard", None),
            P("shard"),
            P("shard", None),
            P("shard"),
        ),
        out_specs=(
            P("shard", "seq", None, None),
            P("shard", "seq", None, None),
            P("shard"),
            P("shard"),
            P("shard", None),
            P(None, "shard"),
            P(None, "shard"),
            P("shard", None),
            P("shard"),
            P("shard"),
            P("shard"),
            P("shard", None),
            P("shard"),
            P("shard", None),
            P("shard"),
        ),
        check_vma=False,
    )
```

time: 778 us -> 304 us (0.39); the launches traced: 768 us -> 304 us
  blocking collectives: 206 us -> 0 us
  local copies, waits for them, and re-layouts: 174 us -> 8.24 us
  Pallas kernels: 0 us -> 93.1 us
  matrix products: 89.7 us -> 0 us
  other arithmetic: 53.5 us -> 2.76 us
  waiting for transfers between devices: 215 us -> 177 us
    all_to_all x3 -> x0, blocking collectives: 118 us -> none  [the longest x1 64.5 us: per_device(): lax.all_to_all(grad_stacked, 'seq', split_axis=2, concat_axis=4, tiled=True)]
    pallas_call x0 -> x5, Pallas kernels: none -> 93.1 us  [kernel_call(): pl.pallas_call(body, out_shape=tuple(outs), in_specs=[whole(pltpu.SMEM)]...]
    dot_general x20 -> x0, matrix products: 89.7 us -> none  [the longest x1 19.5 us: per_device(): jnp.dot(normed_two_low, in_weight, preferred_element_type=jnp.float32)]
    reduce_scatter x4 -> x2, waiting for transfers between devices: 149 us -> 96.7 us  [the longest x1 55.4 us: per_device(): mlp_share = lax.psum_scatter(mlp_grads, 'shard', scatter_dimension=0)]
    all_to_all x1 -> x0, waiting for transfers between devices: 49.8 us -> none  [per_device(): lax.all_to_all(stacked, 'seq', split_axis=4, concat_axis=2, tiled=True)]
    convert_element_type x7 -> x0, local copies, waits for them, and re-layouts: 42.3 us -> none  [the longest x1 18.3 us: per_device(): attended = jnp.einsum('nhqk,nhke->nhqe', attention, value_win, preferred_...]
    unnamed x2 -> x0, blocking collectives: 39.4 us -> none
    all_gather x4 -> x0, blocking collectives: 36 us -> none  [the longest x1 10.6 us: per_device(): lax.all_gather(w_proj, 'shard', axis=0, tiled=True)]
  transfers between devices with their start and end apart: 14 -> 9, of which waited for: 7 -> 8; matrix products, arithmetic and copies ran while one was open for 23% -> 2% of each run, Pallas kernels for 0% -> 10%
where the time goes in v1:
time: 304 us
  waiting for transfers between devices  177 us (58%)
  Pallas kernels  93.1 us (31%)
  between operations  13.9 us (5%)
  starting transfers between devices  8.84 us (3%)
  local copies, waits for them, and re-layouts  8.24 us (3%)
    pallas_call x5, Pallas kernels, kernel_call(): pl.pallas_call(body, out_shape=tuple(outs), in_specs=[whole(pltpu.SMEM)]...  93.1 us
    reduce_scatter x1, waiting for transfers between devices, per_device(): mlp_share = lax.psum_scatter(mlp_grads, 'shard', scatter_dimension=0)  55.4 us
    reduce_scatter x1, waiting for transfers between devices, per_device(): attn_share = lax.psum_scatter(attn_grads, 'shard', scatter_dimension=0)  41.3 us
    ppermute x4, waiting for transfers between devices, shifted_2(): lax.ppermute(value, axis, [(i, (i + by) % peers) for i in range(peers)])  36.7 us
    psum x1, waiting for transfers between devices, per_device(): attn_total, mlp_total = lax.psum((attn_share, mlp_share), 'seq')  24.1 us
    all_gather x1, waiting for transfers between devices, per_device(): attn_all = lax.all_gather(attn_slab, 'shard')  9.7 us
    ppermute x4, starting transfers between devices, shifted_2(): lax.ppermute(value, axis, [(i, (i + by) % peers) for i in range(peers)])  8.64 us
    all_gather x1, waiting for transfers between devices, per_device(): mlp_all = lax.all_gather(mlp_slab, 'shard')  8.51 us
  transfers between devices with their start and end apart: 9, of which 8 were waited for; matrix products, arithmetic and copies ran while one was open for 2% of the time, Pallas kernels for 10%

profile of v1, /device:TPU:0, one launch (start us, length us, event | category | flops | bytes accessed | tf_op | source)
XLA Modules:
  0.0 303.9 jit_solution(2284669894045509157)
XLA Ops:
  7.2 1.2 broadcast_in_dim.39.bin_
  8.5 1.4 copy.38.table
  9.9 2.8 shard_map.271
  12.8 0.7 all-gather.7.cloned.1.call-update
  13.5 1.0 slice_bitcast_fusion
  14.5 5.1 %collective-permute-start.1 = (bf16[3,112,512]{2,1,0:T(8,128)(2,1)S(1)}, bf16[3,112,512]{2,1,0:T(8,128)(2,1)S(1)}, u32[]{:S(2)}, u32[]{:S(2)}) collective-permute-start(bf16[3,112,512]{2,1,0:T(8,128)(2,1)S(1)} %slice_bitcast_fusion), channel_id=1, source_target_pairs={{0,3},{1,0},{2,1},{3,2},{4,7},{5,4},{6,5},{7,6},{8,11},{9,8},{10,9... | collective-permute-start | bytes 1032200 | tf_op jit(solution)/shard_map/ppermute | solution.py:36
  19.6 1.0 slice_bitcast_fusion.1
  20.6 0.5 collective-permute-start
  21.2 0.1 reshape.73
  21.2 0.1 copy.39
  21.5 0.1 copy.41
  21.6 0.6 broadcast_in_dim.44.reg_lanes
  22.2 12.1 %collective-permute-done.halo = bf16[3,112,512]{2,1,0:T(8,128)(2,1)S(1)} collective-permute-done((bf16[3,112,512]{2,1,0:T(8,128)(2,1)S(1)}, bf16[3,112,512]{2,1,0:T(8,128)(2,1)S(1)}, u32[]{:S(2)}, u32[]{:S(2)}) %collective-permute-start) | collective-permute-done | bytes 344096 | tf_op jit(solution)/shard_map/ppermute | solution.py:36
  34.3 9.7 %all-gather.5.cloned.1.call-done = bf16[2176,512]{1,0:T(8,128)(2,1)} async-done(((bf16[272,512]{1,0:T(8,128)(2,1)}), bf16[2176,512]{1,0:T(8,128)(2,1)}) %all-gather.5.cloned.1.call-update) | async-done | bytes 2228240 | tf_op jit(solution)/shard_map/all_gather | solution.py:583
  44.0 1.0 broadcast_in_dim.42.reg_rows
  45.0 30.4 %shard_map.272 = (f32[784,512]{1,0:T(8,128)}, bf16[896,512]{1,0:T(8,128)(2,1)}, bf16[896,512]{1,0:T(8,128)(2,1)}, bf16[896,512]{1,0:T(8,128)(2,1)}, bf16[896,512...) custom-call(bf16[7,112,512]{2,1,0:T(8,128)(2,1)} %bitcast.36, ...), custom_call_target="tpu_custom_call" | custom-call | flops 5000000000 | bytes 11780096 | tf_op jit(solution)/shard_map/pallas_call | solution.py:125
  75.4 8.5 %all-gather.7.cloned.1.call-done = bf16[4224,512]{1,0:T(8,128)(2,1)} async-done(((bf16[528,512]{1,0:T(8,128)(2,1)}), bf16[4224,512]{1,0:T(8,128)(2,1)}) %all-gather.7.cloned.1.call-update) | async-done | bytes 4325392 | tf_op jit(solution)/shard_map/all_gather | solution.py:584
  83.9 21.6 %shard_map.273 = (f32[448,512]{1,0:T(8,128)}, bf16[336,512]{1,0:T(8,128)(2,1)}, f32[784,512]{1,0:T(8,128)}, bf16[8,528,512]{2,1,0:T(8,128)(2,1)}) custom-call(f32[784,512]{1,0:T(8,128)} %get-tuple-element.45.mixed, bf16[7,112,512]{2,1,0:T(8,128)(2,1)} %bitcast.35, bf16[3,112,512]{2,1,0:T(8,128)(2,1)} %copy-done.4, bf16[8,528,512]{2,1,0:T(8,128)(2,1)} %bitcast.45), custom_call_target="tpu_custom_call" | custom-call | flops 10000000000 | bytes 14270464 | tf_op jit(solution)/shard_map/pallas_call | solution.py:125
  105.5 35.3 %shard_map.274 = (f32[448,512]{1,0:T(8,128)}, bf16[336,512]{1,0:T(8,128)(2,1)}, bf16[8,272,512]{2,1,0:T(8,128)(2,1)}) custom-call(f32[784,512]{1,0:T(8,128)} %get-tuple-element.49.grad_mixed, bf16[7,112,512]{2,1,0:T(8,128)(2,1)} %bitcast.37, bf16[3,112,512]{2,1,0:T(8,128)(2,1)} %copy-done.3, bf16[8,272,512]{2,1,0:T(8,128)(2,1)} %bitcast.47, ...), custom_call_target="tpu_custom_call" | custom-call | flops 10000000000 | bytes 14778368 | tf_op jit(solution)/shard_map/pallas_call | solution.py:125
  140.9 0.5 reduce-scatter.5.cloned.1.call-update
  141.5 41.3 %reduce-scatter.3.cloned.1.call-done = bf16[1,272,512]{2,1,0:T(8,128)(2,1)} async-done(((bf16[8,272,512]{2,1,0:T(8,128)(2,1)}), bf16[1,272,512]{2,1,0:T(8,128)(2,1)}) %reduce-scatter.3.cloned.1.call-update) | async-done | bytes 278544 | tf_op jit(solution)/shard_map/reduce_scatter | solution.py:660
  182.8 55.4 %reduce-scatter.5.cloned.1.call-done = bf16[1,528,512]{2,1,0:T(8,128)(2,1)} async-done(((bf16[8,528,512]{2,1,0:T(8,128)(2,1)}), bf16[1,528,512]{2,1,0:T(8,128)(2,1)}) %reduce-scatter.5.cloned.1.call-update) | async-done | bytes 540688 | tf_op jit(solution)/shard_map/reduce_scatter | solution.py:629
  238.2 1.6 collective-permute-start.2
  239.8 1.5 collective-permute-start.3
  241.3 11.0 %collective-permute-done.2 = bf16[336,512]{1,0:T(8,128)(2,1)S(1)} collective-permute-done((bf16[336,512]{1,0:T(8,128)(2,1)S(1)}, bf16[336,512]{1,0:T(8,128)(2,1)S(1)}, u32[]{:S(2)}, u32[]{:S(2)}) %collective-permute-start.2) | collective-permute-done | bytes 344096 | tf_op jit(solution)/shard_map/ppermute | solution.py:36
  252.3 0.1 convert_element_type.12
  252.4 13.6 %collective-permute-done.3 = bf16[336,512]{1,0:T(8,128)(2,1)S(1)} collective-permute-done((bf16[336,512]{1,0:T(8,128)(2,1)S(1)}, bf16[336,512]{1,0:T(8,128)(2,1)S(1)}, u32[]{:S(2)}, u32[]{:S(2)}) %collective-permute-start.3) | collective-permute-done | bytes 344096 | tf_op jit(solution)/shard_map/ppermute | solution.py:36
  266.0 1.3 pad_maximum_fusion
  267.4 1.3 pad_maximum_fusion.1
  268.6 24.1 %all-reduce.5.cloned.1.call-done = (bf16[272,512]{1,0:T(8,128)(2,1)}, bf16[528,512]{1,0:T(8,128)(2,1)}) async-done(((bf16[272,512]{1,0:T(8,128)(2,1)}, bf16[528,512]{1,0:T(8,128)(2,1)}), (bf16[272,512]{1,0:T(8,128)(2,1)}, bf16[528,512]{1,0:T(8,128)(2,1)})) %all-reduce.5.cloned.1.call-update) | async-done | bytes 819216 | tf_op jit(solution)/shard_map/psum | solution.py:662
  292.7 3.1 %shard_map.275 = (f32[1,64]{1,0:T(1,128)}, f32[1,64]{1,0:T(1,128)}, f32[64,1536]{1,0:T(8,128)}, f32[2,64]{1,0:T(2,128)}, f32[169,2]{1,0:T(8,128)}, /*index=5*/f3...) custom-call(s32[1]{0:T(128)} %bitcast.2.me_ref, ...), custom_call_target="tpu_custom_call" | custom-call | bytes 2396492 | tf_op jit(solution)/shard_map/pallas_call | solution.py:125
  295.8 1.5 copy.42
  (29 shorter events, 0.5 us)
Async XLA Ops:
  7.2 14.0 %copy-start = (s32[1,28,112]{2,0,1:T(1,128)S(1)}, s32[1,28,112]{2,0,1:T(1,128)}, u32[]{:S(2)}) copy-start(s32[1,28,112]{2,0,1:T(1,128)} %param.17) | copy-start | bytes 37636
  7.2 36.8 %all-gather.5.cloned.1.call-start = ((), (), s32[]{:S(2)}) async-start(), calls=%async_computation.4 | async-start | bytes 2506752 | tf_op jit(solution)/shard_map/all_gather | solution.py:583
  12.7 71.2 %all-gather.7.cloned.1.call-start = ((), (), s32[]{:S(2)}) async-start(), calls=%async_computation.5 | async-start | bytes 4866048 | tf_op jit(solution)/shard_map/all_gather | solution.py:584
  13.5 169.3 %reduce-scatter.3.cloned.1.call-start = ((), (), s32[]{:S(2)}) async-start(), calls=%async_computation.2 | async-start | bytes 2506752 | tf_op jit(solution)/shard_map/reduce_scatter | solution.py:660
  14.5 60.8 %collective-permute-start.1 = (bf16[3,112,512]{2,1,0:T(8,128)(2,1)S(1)}, bf16[3,112,512]{2,1,0:T(8,128)(2,1)S(1)}, u32[]{:S(2)}, u32[]{:S(2)}) collective-permute-start(bf16[3,112,512]{2,1,0:T(8,128)(2,1)S(1)} %slice_bitcast_fusion), channel_id=1, source_target_pairs={{0,3},{1,0},{2,1},{3,2},{4,7},{5,4},{6,5},{7,6},{8,11},{9,8},{10,9... | collective-permute-start | bytes 1032200 | tf_op jit(solution)/shard_map/ppermute | solution.py:36
  20.6 13.7 %collective-permute-start = (bf16[3,112,512]{2,1,0:T(8,128)(2,1)S(1)}, bf16[3,112,512]{2,1,0:T(8,128)(2,1)S(1)}, u32[]{:S(2)}, u32[]{:S(2)}) collective-permute-start(bf16[3,112,512]{2,1,0:T(8,128)(2,1)S(1)} %slice_bitcast_fusion.1), channel_id=1, source_target_pairs={{0,3},{1,0},{2,1},{3,2},{4,7},{5,4},{6,5},{7,6},{8,11},{9,8},{10,9... | collective-permute-start | bytes 1032200 | tf_op jit(solution)/shard_map/ppermute | solution.py:36
  34.3 10.7 %copy-start.3 = (bf16[3,112,512]{2,1,0:T(8,128)(2,1)}, bf16[3,112,512]{2,1,0:T(8,128)(2,1)S(1)}, u32[]{:S(2)}) copy-start(bf16[3,112,512]{2,1,0:T(8,128)(2,1)S(1)} %collective-permute-done.halo) | copy-start | bytes 1032196
  75.4 8.5 %copy-start.4 = (bf16[3,112,512]{2,1,0:T(8,128)(2,1)}, bf16[3,112,512]{2,1,0:T(8,128)(2,1)S(1)}, u32[]{:S(2)}) copy-start(bf16[3,112,512]{2,1,0:T(8,128)(2,1)S(1)} %collective-permute-done.1.halo) | copy-start | bytes 1032196
  140.8 97.4 %reduce-scatter.5.cloned.1.call-start = ((), (), s32[]{:S(2)}) async-start(), calls=%async_computation.3 | async-start | bytes 4866048 | tf_op jit(solution)/shard_map/reduce_scatter | solution.py:629
  140.9 97.3 %copy-start.5 = (bf16[336,512]{1,0:T(8,128)(2,1)S(1)}, bf16[336,512]{1,0:T(8,128)(2,1)}, u32[]{:S(2)}) copy-start(bf16[336,512]{1,0:T(8,128)(2,1)} %get-tuple-element.47) | copy-start | bytes 1032196
  140.9 98.9 %copy-start.6 = (bf16[336,512]{1,0:T(8,128)(2,1)S(1)}, bf16[336,512]{1,0:T(8,128)(2,1)}, u32[]{:S(2)}) copy-start(bf16[336,512]{1,0:T(8,128)(2,1)} %get-tuple-element.56) | copy-start | bytes 1032196
  141.4 124.6 %copy-start.1 = (f32[448,512]{1,0:T(8,128)S(1)}, f32[448,512]{1,0:T(8,128)}, u32[]{:S(2)}) copy-start(f32[448,512]{1,0:T(8,128)} %get-tuple-element.48) | copy-start | bytes 2752516
  141.4 151.3 %all-reduce.5.cloned.1.call-start = ((), (), s32[]{:S(2)}) async-start(), calls=%async_computation.6 | async-start | bytes 1638400 | tf_op jit(solution)/shard_map/psum | solution.py:662
  238.2 14.1 %collective-permute-start.2 = (bf16[336,512]{1,0:T(8,128)(2,1)S(1)}, bf16[336,512]{1,0:T(8,128)(2,1)S(1)}, u32[]{:S(2)}, u32[]{:S(2)}) collective-permute-start(bf16[336,512]{1,0:T(8,128)(2,1)S(1)} %copy-done.5), channel_id=1, source_target_pairs={{0,1},{1,2},{2,3},{3,0},{4,5},{5,6},{6,7},{7,4},{8,9},{9,10},{10,1... | collective-permute-start | bytes 1032200 | tf_op jit(solution)/shard_map/ppermute | solution.py:36
  239.8 26.1 %collective-permute-start.3 = (bf16[336,512]{1,0:T(8,128)(2,1)S(1)}, bf16[336,512]{1,0:T(8,128)(2,1)S(1)}, u32[]{:S(2)}, u32[]{:S(2)}) collective-permute-start(bf16[336,512]{1,0:T(8,128)(2,1)S(1)} %copy-done.6), channel_id=1, source_target_pairs={{0,1},{1,2},{2,3},{3,0},{4,5},{5,6},{6,7},{7,4},{8,9},{9,10},{10,1... | collective-permute-start | bytes 1032200 | tf_op jit(solution)/shard_map/ppermute | solution.py:36
  266.0 1.3 copy-start.2
Sparse Core Ops, SparseCore 0:
  12.8 31.1 all-gather.4
  46.5 37.3 all-gather.6
  141.0 41.8 reduce-scatter.2
  186.1 52.0 reduce-scatter.4
  240.5 52.2 all-reduce.4

commit v2 on v1

--- a/solution.py
+++ b/solution.py
@@ -23,7 +23,7 @@
 PADDED = WINDOWS * PLACES
 TAB = 1536
 TAB_USED = 768
-SMALL = 16
+SMALL = 32
 EPS = 1e-05
 SCALE = HEAD**-0.5
 BF = jnp.bfloat16
@@ -120,12 +120,14 @@
     return pl.BlockSpec(memory_space=memory)
 
 
-def kernel_call(body, outs, ins, scratch=(), flops=0, smem=0):
+def kernel_call(body, outs, ins, scratch=(), flops=0, smem=0, apart=0):
     size = sum(a.size * a.dtype.itemsize for a in list(ins) + list(outs))
     return pl.pallas_call(
         body,
         out_shape=tuple(outs),
-        in_specs=[whole(pltpu.SMEM)] * smem + [whole()] * (len(ins) - smem),
+        in_specs=[whole(pltpu.SMEM)] * smem
+        + [whole()] * (len(ins) - smem - apart)
+        + [whole(pl.ANY)] * apart,
         out_specs=tuple(whole() for _ in outs),
         scratch_shapes=list(scratch),
         cost_estimate=pl.CostEstimate(flops=flops, bytes_accessed=size, transcendentals=0),
@@ -137,34 +139,39 @@
     return jax.ShapeDtypeStruct(shape, dtype)
 
 
-def pack_body(
-    me_ref, g1, b1, wqkv, bqv, table, wproj, bproj, g2, b2, win, bin_, wout, bout, attn, mlp
-):
+def place(vector, lanes, me):
+    w = vector.shape[1]
+    pick = one_hot(iota((w, lanes), 1) == iota((w, lanes), 0) + me * w)
+    wide = jnp.broadcast_to(vector, (8, w))
+    return dot(wide.astype(BF), pick)[0:1]
+
+
+def mine(row, w, me):
+    lanes = row.shape[1]
+    pick = one_hot(iota((lanes, w), 0) == iota((lanes, w), 1) + me * w)
+    wide = jnp.broadcast_to(row, (8, lanes))
+    return dot(wide.astype(BF), pick)[0:1]
+
+
+def padded(rows, height):
+    total = sum(r.shape[0] for r in rows)
+    return jnp.concatenate(rows + [jnp.zeros((height - total, D), F32)], 0).astype(BF)
+
+
+def pack_attn_body(me_ref, g1, b1, wqkv, bqv, table, wproj, bproj, attn):
     depth = wqkv.shape[0]
     me = me_ref[0]
-
-    def place(vector, lanes):
-        w = vector.shape[1]
-        pick = one_hot(iota((w, lanes), 1) == iota((w, lanes), 0) + me * w)
-        wide = jnp.broadcast_to(vector, (8, w))
-        return dot(wide.astype(BF), pick)[0:1]
-
     for c in range(3):
         attn[c * depth : (c + 1) * depth, :] = wqkv[:, c * D : (c + 1) * D]
     attn[3 * depth : 4 * depth, :] = wproj[...]
     rows = [
-        place(g1[...], D),
-        place(b1[...], D),
-        place(bqv[0:1, :], D),
-        place(bqv[1:2, :], D),
-        place(bproj[...], D),
+        place(v, D, me) for v in (g1[...], b1[...], bqv[0:1, :], bqv[1:2, :], bproj[...])
     ]
-    entries, held = table.shape
+    held, entries = table.shape
     lane = iota((entries, TAB), 1)
-    entry = iota((entries, TAB), 0)
-    spot = entry * GROUP + TAB - (WIN - 1) * 2 * WIN * GROUP
+    spot = iota((entries, TAB), 0) * GROUP + TAB - (WIN - 1) * 2 * WIN * GROUP
     spot = jnp.where(spot >= TAB, spot - TAB, spot)
-    values = table[...].astype(F32)
+    values = table[...].astype(F32).T
     groups = [jnp.zeros((1, TAB), F32) for _ in range(GROUPS)]
     for h in range(held):
         head = me * held + h
@@ -174,47 +181,63 @@
             groups[g] = groups[g] + jnp.where((head >> 3) == g, row, 0.0)
     for g in range(GROUPS):
         rows += [groups[g][:, c * D : (c + 1) * D] for c in range(TAB // D)]
-    rows += [jnp.zeros((SMALL - len(rows), D), F32)]
-    attn[4 * depth :, :] = jnp.concatenate(rows, 0).astype(BF)
-
+    attn[4 * depth :, :] = padded(rows, SMALL)
+
+
+def pack_mlp_body(me_ref, g2, b2, win, bin_, wout, bout, mlp):
+    depth = win.shape[0]
+    me = me_ref[0]
     for c in range(FF // D):
         mlp[c * depth : (c + 1) * depth, :] = win[:, c * D : (c + 1) * D]
     mlp[4 * depth : 8 * depth, :] = wout[...]
-    hidden_bias = place(bin_[...], FF)
-    rows = [place(g2[...], D), place(b2[...], D), place(bout[...], D)]
+    hidden_bias = place(bin_[...], FF, me)
+    rows = [place(v, D, me) for v in (g2[...], b2[...], bout[...])]
     rows += [hidden_bias[:, c * D : (c + 1) * D] for c in range(FF // D)]
-    rows += [jnp.zeros((SMALL - len(rows), D), F32)]
-    mlp[8 * depth :, :] = jnp.concatenate(rows, 0).astype(BF)
+    mlp[8 * depth :, :] = padded(rows, SMALL)
 
 
 def unpack_body(
-    me_ref, attn, mlp, g1, b1, wqkv, bqv, table, wproj, bproj, g2, b2, win, bin_, wout, bout
+    me_ref,
+    attn_half,
+    attn_back,
+    mlp_half,
+    mlp_back,
+    g1,
+    b1,
+    wqkv,
+    bqv,
+    table,
+    wproj,
+    bproj,
+    g2,
+    b2,
+    win,
+    bin_,
+    wout,
+    bout,
+    attn,
+    mlp,
 ):
     depth = wqkv.shape[0]
     me = me_ref[0]
-
-    def mine(row, w):
-        lanes = row.shape[1]
-        pick = one_hot(iota((lanes, w), 0) == iota((lanes, w), 1) + me * w)
-        wide = jnp.broadcast_to(row, (8, lanes))
-        return dot(wide.astype(BF), pick)[0:1]
-
+    late = me_ref[1]
+    for half, back, both in ((attn_half, attn_back, attn), (mlp_half, mlp_back, mlp)):
+        rows = half.shape[0]
+        both[pl.ds(pl.multiple_of(late * rows, 16), rows), :] = half[...]
+        both[pl.ds(pl.multiple_of((1 - late) * rows, 16), rows), :] = back[...]
     for c in range(3):
         wqkv[:, c * D : (c + 1) * D] = attn[c * depth : (c + 1) * depth, :].astype(F32)
-    wproj[...] = attn[3 * depth : 4 * depth, :].astype(F32)
-    small = attn[4 * depth :, :].astype(F32)
-    w = D * depth // D
-    g1[...] = mine(small[0:1], w)
-    b1[...] = mine(small[1:2], w)
-    bqv[0:1, :] = mine(small[2:3], w)
-    bqv[1:2, :] = mine(small[3:4], w)
-    bproj[...] = mine(small[4:5], w)
-    entries, held = table.shape
+    small = attn[3 * depth :, :].astype(F32)
+    g1[...] = mine(small[0:1], depth, me)
+    b1[...] = mine(small[1:2], depth, me)
+    bqv[0:1, :] = mine(small[2:3], depth, me)
+    bqv[1:2, :] = mine(small[3:4], depth, me)
+    held, entries = table.shape
     lane = iota((entries, TAB), 1)
     spot = (entries - 1 - iota((entries, TAB), 0)) * GROUP
     parts = TAB // D
     rows = [
-        jnp.concatenate([small[5 + g * parts + c : 6 + g * parts + c] for c in range(parts)], 1)
+        jnp.concatenate([small[4 + g * parts + c : 5 + g * parts + c] for c in range(parts)], 1)
         for g in range(GROUPS)
     ]
     which = iota((entries, held), 1)
@@ -227,18 +250,93 @@
         inside = lane == spot + (head & (GROUP - 1))
         column = jnp.sum(jnp.where(inside, row, 0.0), 1, keepdims=True)
         total = jnp.where(which == h, column, total)
-    table[...] = total
+    table[...] = total.T
 
     for c in range(FF // D):
         win[:, c * D : (c + 1) * D] = mlp[c * depth : (c + 1) * depth, :].astype(F32)
     wout[...] = mlp[4 * depth : 8 * depth, :].astype(F32)
-    small = mlp[8 * depth :, :].astype(F32)
-    g2[...] = mine(small[0:1], w)
-    b2[...] = mine(small[1:2], w)
-    bout[...] = mine(small[2:3], w)
-    bin_[...] = mine(
-        jnp.concatenate([small[3 + c : 4 + c] for c in range(FF // D)], 1), w * FF // D
-    )
+    wproj[...] = mlp[8 * depth : 9 * depth, :].astype(F32)
+    small = mlp[9 * depth :, :].astype(F32)
+    g2[...] = mine(small[0:1], depth, me)
+    b2[...] = mine(small[1:2], depth, me)
+    bout[...] = mine(small[2:3], depth, me)
+    bproj[...] = mine(small[3:4], depth, me)
+    hidden = jnp.concatenate([small[4 + c : 5 + c] for c in range(FF // D)], 1)
+    bin_[...] = mine(hidden, depth * FF // D, me)
+
+
+def put_shares(me, same, other, start, values, first=0):
+    core, chip = me & 1, me >> 1
+    rows = values.shape[1]
+    for c in range(values.shape[0] // 2):
+        one, two = values[2 * c], values[2 * c + 1]
+        q = (first // 2 + c) ^ chip
+        same[q, start : start + rows, :] = jnp.where(core == 0, one, two).astype(BF)
+        other[q, start : start + rows, :] = jnp.where(core == 0, two, one).astype(BF)
+
+
+def put_smalls(same, other, start, rows):
+    block = padded(rows, SMALL)
+    for q in range(same.shape[0]):
+        same[q, start:, :] = block
+        other[q, start:, :] = block
+
+
+def add_cores_body(same, came, *sums):
+    for q, total in enumerate(sums):
+        total[...] = (same[q].astype(F32) + came[q].astype(F32)).astype(BF)
+
+
+def add_chips_body(me_ref, *refs):
+    parts, (keep, send) = refs[:-2], refs[-2:]
+    half = keep.shape[0]
+    late = me_ref[1]
+    for place_at, target in ((late, keep), (1 - late, send)):
+        rows = pl.ds(pl.multiple_of(place_at * half, 16), half)
+        total = parts[0][rows, :].astype(F32)
+        for part in parts[1:]:
+            total += part[rows, :].astype(F32)
+        target[...] = total.astype(BF)
+
+
+def exchange(value, axis, mask):
+    peers = lax.axis_size(axis)
+    return lax.ppermute(value, axis, [(i, i ^ mask) for i in range(peers)])
+
+
+def gather_pieces(slab):
+    chips = lax.axis_size("shard") // 2
+    pieces = [None] * (2 * chips)
+    for q in range(chips):
+        pieces[2 * q] = exchange(slab, "shard", 2 * q) if q else slab
+    for q in range(chips):
+        pieces[2 * q + 1] = exchange(pieces[2 * q], "shard", 1)
+    return pieces
+
+
+def add_cores(same, other):
+    came = exchange(other, "shard", 1)
+    chips, rows, _ = same.shape
+    return kernel_call(add_cores_body, [like((rows, D), BF)] * chips, (same, came))
+
+
+def add_chips(where, sums):
+    parts = [sums[0]] + [exchange(sums[q], "shard", 2 * q) for q in range(1, len(sums))]
+    rows = sums[0].shape[0]
+    return kernel_call(add_chips_body, [like((rows // 2, D), BF)] * 2, (where, *parts), smem=1)
+
+
+def add_pair(here, came):
+    return (here.astype(F32) + came.astype(F32)).astype(BF)
+
+
+def add_seq(keep, send):
+    half = add_pair(keep, exchange(send, "seq", 1))
+    reach = 2
+    while reach < lax.axis_size("seq"):
+        half = add_pair(half, exchange(half, "seq", reach))
+        reach *= 2
+    return half, exchange(half, "seq", 1)
 
 
 def block_of(slab, c, depth):
@@ -249,26 +347,38 @@
     return jnp.sum(slab[:, start:, :].astype(F32), 0)
 
 
-def attn_forward_body(
-    tokens,
-    halo,
-    slab,
-    reg_rows,
-    reg_lanes,
-    mixed,
-    normed_win,
-    query,
-    key,
-    value,
-    probs,
-    restored,
-    wide,
-    spread,
-    fold,
-    mask,
-    bias,
-):
+def load_pieces(me, pieces, slab, sems):
+    copies = [
+        pltpu.make_async_copy(piece, slab.at[me ^ p], sems.at[p]) for p, piece in enumerate(pieces)
+    ]
+    for copy in copies:
+        copy.start()
+    return copies
+
+
+def attn_forward_body(me_ref, tokens, halo, reg_rows, reg_lanes, *refs):
+    shards = len(refs) - 14
+    pieces = refs[:shards]
+    (
+        mixed,
+        normed_win,
+        query,
+        key,
+        value,
+        probs,
+        restored,
+        slab,
+        wide,
+        spread,
+        fold,
+        mask,
+        bias,
+        sems,
+    ) = refs[shards:]
+    copies = load_pieces(me_ref[0], pieces, slab, sems)
     depth = (slab.shape[1] - SMALL) // 4
+    for copy in copies:
+        copy.wait()
     small = smalls_of(slab, 4 * depth)
     gain, offset = small[0:1], small[1:2]
     bias_q, bias_v, bias_o = small[2:3], small[3:4], small[4:5]
@@ -351,8 +461,26 @@
 
 
 def mlp_body(
-    mixed, cotangent, halo, slab, kept, sent, grad_mixed, grads, normed_low, cot, out_sum, back_sum
+    me_ref,
+    mixed,
+    cotangent,
+    halo,
+    slab,
+    attn_slab,
+    restored,
+    kept,
+    sent,
+    grad_mixed,
+    grad_win,
+    same,
+    other,
+    normed_low,
+    cot,
+    out_sum,
+    back_sum,
+    wide,
 ):
+    me = me_ref[0]
     shards, height = slab.shape[:2]
     depth = (height - SMALL) // 8
     span = shards * D // FF
@@ -382,70 +510,43 @@
             out_sum[...] += forward
             back_sum[...] += backward
         vectors.append(jnp.sum(grad.astype(F32), 0, keepdims=True))
-        grads[:, c * depth : (c + 1) * depth, :] = (
-            dot_tn(normed_low[...], grad).astype(BF).reshape(shards, depth, D)
+        put_shares(
+            me, same, other, c * depth, dot_tn(normed_low[...], grad).reshape(shards, depth, D)
         )
-        grads[c * span : (c + 1) * span, 4 * depth : 8 * depth, :] = (
-            dot_tn(active, cot[...]).astype(BF).reshape(span, 4 * depth, D)
+        put_shares(
+            me,
+            same,
+            other,
+            4 * depth,
+            dot_tn(active, cot[...]).reshape(span, 4 * depth, D),
+            c * span,
         )
     result = mixed[...] + out_sum[...] + bias_o
     kept[...] = result[: own * WIDTH]
     sent[...] = result[own * WIDTH :].astype(BF)
     normed, scale = norm_stats(mixed[...])
     g = back_sum[...]
-    rows = [
-        jnp.sum(g * normed, 0, keepdims=True),
-        jnp.sum(g, 0, keepdims=True),
-        jnp.sum(cot[...].astype(F32), 0, keepdims=True),
-    ] + vectors
-    rows += [jnp.zeros((SMALL - len(rows), D), F32)]
-    grads[:, 8 * depth :, :] = jnp.broadcast_to(
-        jnp.concatenate(rows, 0).astype(BF)[None], (shards, SMALL, D)
-    )
+    gain_sum = jnp.sum(g * normed, 0, keepdims=True)
+    offset_sum = jnp.sum(g, 0, keepdims=True)
+    cot_sum = jnp.sum(cot[...].astype(F32), 0, keepdims=True)
     grad_mixed[...] = cot[...].astype(F32) + norm_back(g, normed, scale, gain)
 
-
-def attn_backward_body(
-    grad_mixed,
-    tokens,
-    halo,
-    slab,
-    normed_win,
-    query,
-    key,
-    value,
-    probs,
-    restored,
-    kept,
-    sent,
-    grads,
-    wide,
-    grad_qkv,
-    spread,
-    fold,
-    mask,
-    pairs,
-):
-    shards = slab.shape[0]
-    depth = (slab.shape[1] - SMALL) // 4
-    small = smalls_of(slab, 4 * depth)
-    gain = small[0:1]
+    branch = grad_mixed[...].astype(BF)
+    branch_sum = jnp.sum(branch.astype(F32), 0, keepdims=True)
+    proj = dot_tn(restored[...], branch).reshape(shards, depth, D)
+    put_shares(me, same, other, 8 * depth, proj)
+    put_smalls(same, other, 9 * depth, [gain_sum, offset_sum, cot_sum, branch_sum] + vectors)
+    grad_att = dot_nt(branch, block_of(attn_slab, 3, depth)).astype(BF)
+    columns = column_places()
+    for r in range(WIN):
+        wide[:, r] = dot(columns, grad_att[r * WIDTH : (r + 1) * WIDTH]).reshape(WINDOWS, SLOT, D)
+    grad_win[...] = wide[...].reshape(PADDED, D).astype(BF)
+
+
+def attn_pairs(first, last, query, key, value, probs, grad_win, out, spread, fold, mask, pairs):
     spread[...] = spread_matrix()
     fold[...] = fold_matrix()
     mask[...] = head_mask(1.0)
-    pairs[...] = jnp.zeros_like(pairs)
-    own = WIN - SHIFT
-
-    def store(c, grad):
-        grads[:, c * depth : (c + 1) * depth, :] = grad.astype(BF).reshape(shards, depth, D)
-
-    branch = grad_mixed[...].astype(BF)
-    bias_o = jnp.sum(branch.astype(F32), 0, keepdims=True)
-    store(3, dot_tn(restored[...], branch))
-    grad_att = dot_nt(branch, block_of(slab, 3, depth)).astype(BF)
-    columns = column_places()
-    for r in range(WIN):
-        wide[:, r] = dot(columns, grad_att[r * WIDTH : (r + 1) * WIDTH]).reshape(WINDOWS, SLOT, D)
 
     def pair(n, carry):
         rows = pl.ds(pl.multiple_of(n * 2 * PLACES, 2 * PLACES), 2 * PLACES)
@@ -454,14 +555,13 @@
             q2 = query[rows, feats].astype(F32)
             k2 = key[rows, feats].astype(F32)
             v2 = value[rows, feats].astype(F32)
+            go2 = grad_win[rows, feats].astype(F32)
             p2 = probs[n, g].astype(F32)
             held = []
             for s in range(2):
-                w = 2 * n + s
                 part = slice(s * PLACES, (s + 1) * PLACES)
-                q, k, v, p_low = (a[part].astype(BF) for a in (q2, k2, v2, p2))
+                q, k, v, go, p_low = (a[part].astype(BF) for a in (q2, k2, v2, go2, p2))
                 p = p2[part]
-                go = wide[w, :, :, feats].reshape(PLACES, FEAT).astype(BF)
                 go_big = (dot(spread[...], go) * mask[...]).astype(BF)
                 q_big = (dot(spread[...], q) * mask[...]).astype(BF)
                 dp = dot_nt(v, go_big)
@@ -473,18 +573,77 @@
                 dq_big = (dot_tn(ds, k) * (mask[...] * SCALE)).astype(BF)
                 dq = dot(fold[...], dq_big)
                 held.append((dq, dk, dv))
+            to = pl.ds(pl.multiple_of((n - first) * 2 * PLACES, 2 * PLACES), 2 * PLACES)
             for c in range(3):
                 both = jnp.concatenate([held[0][c], held[1][c]], 0).astype(BF)
-                grad_qkv[rows, c * D + g * FEAT : c * D + (g + 1) * FEAT] = both
+                out[to, c * D + g * FEAT : c * D + (g + 1) * FEAT] = both
         return carry
 
-    lax.fori_loop(0, WINDOWS // 2, pair, 0)
+    lax.fori_loop(first, last, pair, 0)
+
+
+def attn_first_body(query, key, value, probs, grad_win, out, pairs, spread, fold, mask):
+    pairs[...] = jnp.zeros_like(pairs)
+    last = out.shape[0] // (2 * PLACES)
+    attn_pairs(0, last, query, key, value, probs, grad_win, out, spread, fold, mask, pairs)
+
+
+def attn_last_body(
+    me_ref,
+    query,
+    key,
+    value,
+    probs,
+    grad_win,
+    grad_early,
+    pairs_early,
+    grad_mixed,
+    tokens,
+    halo,
+    slab,
+    normed_win,
+    kept,
+    sent,
+    same,
+    other,
+    grad_late,
+    spread,
+    fold,
+    mask,
+    pairs,
+    wide,
+):
+    me = me_ref[0]
+    pairs[...] = pairs_early[...]
+    early = grad_early.shape[0]
+    attn_pairs(
+        early // (2 * PLACES),
+        WINDOWS // 2,
+        query,
+        key,
+        value,
+        probs,
+        grad_win,
+        grad_late,
+        spread,
+        fold,
+        mask,
+        pairs,
+    )
+    shards = slab.shape[0]
+    depth = (slab.shape[1] - SMALL) // 4
+    small = smalls_of(slab, 4 * depth)
+    gain = small[0:1]
+    own = WIN - SHIFT
     vectors = []
     for c in range(3):
-        g = grad_qkv[:, c * D : (c + 1) * D]
+        cols = slice(c * D, (c + 1) * D)
+        g = jnp.concatenate([grad_early[:, cols], grad_late[:, cols]], 0)
         if c != 1:
             vectors.append(jnp.sum(g.astype(F32), 0, keepdims=True))
-        store(c, dot_tn(normed_win[...], g))
+        put_shares(
+            me, same, other, c * depth, dot_tn(normed_win[...], g).reshape(shards, depth, D)
+        )
         part = dot_nt(g, block_of(slab, c, depth))
         total = part if c == 0 else total + part
     wide[...] = total.reshape(WINDOWS, WIN, SLOT, D)
@@ -505,7 +664,7 @@
             sent[(r - own) * WIDTH : (r - own + 1) * WIDTH, :] = grad.astype(BF)
 
     pick = table_pick(1, True)
-    rows = [gain_sum, bias_sum, vectors[0], vectors[1], bias_o]
+    rows = [gain_sum, bias_sum, vectors[0], vectors[1]]
     for g in range(GROUPS):
         high = pairs[g].astype(BF)
         low = (pairs[g] - high.astype(F32)).astype(BF)
@@ -519,10 +678,7 @@
         total = pltpu.roll(total, 0, 1, stride=GROUP, stride_axis=0)
         row = jnp.sum(total, 0, keepdims=True)
         rows += [row[:, c * D : (c + 1) * D] for c in range(TAB // D)]
-    rows += [jnp.zeros((SMALL - len(rows), D), F32)]
-    grads[:, 4 * depth :, :] = jnp.broadcast_to(
-        jnp.concatenate(rows, 0).astype(BF)[None], (shards, SMALL, D)
-    )
+    put_smalls(same, other, 3 * depth, rows)
 
 
 def region_views(regions, rows, place):
@@ -556,39 +712,37 @@
     images, local_rows, columns, _ = tokens.shape
     assert images == 1 and local_rows == WIN and columns == WIDTH
     shards = lax.axis_size("shard")
-    me = lax.axis_index("shard").astype(jnp.int32).reshape(1)
+    me = lax.axis_index("shard").astype(jnp.int32)
+    seq = lax.axis_index("seq").astype(jnp.int32)
+    where = jnp.stack([me, seq & 1])
+    chips = shards // 2
     depth = D // shards
     own = WIN - SHIFT
-    params = (
+    attn_params = (
         gain_one[None],
         bias_one[None],
         w_qkv,
         bias_qv,
-        table,
+        table.T,
         w_proj,
         bias_proj[None],
-        gain_two[None],
-        bias_two[None],
-        w_in,
-        bias_in[None],
-        w_out,
-        bias_out[None],
-    )
-    attn_slab, mlp_slab = kernel_call(
-        pack_body,
-        [like((4 * depth + SMALL, D), BF), like((8 * depth + SMALL, D), BF)],
-        (me,) + params,
-        smem=1,
-    )
-    attn_all = lax.all_gather(attn_slab, "shard")
+    )
+    mlp_params = (gain_two[None], bias_two[None], w_in, bias_in[None], w_out, bias_out[None])
+    (attn_slab,) = kernel_call(
+        pack_attn_body, [like((4 * depth + SMALL, D), BF)], (where,) + attn_params, smem=1
+    )
+    pieces = gather_pieces(attn_slab)
+    (mlp_slab,) = kernel_call(
+        pack_mlp_body, [like((8 * depth + SMALL, D), BF)], (where,) + mlp_params, smem=1
+    )
     mlp_all = lax.all_gather(mlp_slab, "shard")
     tokens_here = tokens[0]
     token_halo = shifted_2(tokens_here[:SHIFT], "seq", -1)
     cot_here = cotangent[0]
     cot_halo = shifted_2(cot_here[:SHIFT], "seq", -1)
-    by_row, by_lane = region_views(regions, local_rows, lax.axis_index("seq"))
-
-    mixed, normed_win, query, key, value, probs, restored = kernel_call(
+    by_row, by_lane = region_views(regions, local_rows, seq)
+
+    mixed, normed_win, query, key, value, probs, restored, attn_all = kernel_call(
         attn_forward_body,
         [
             like((TOKENS, D), F32),
@@ -598,92 +752,127 @@
             like((PADDED, D), BF),
             like((WINDOWS // 2, GROUPS, 2 * PLACES, LANES), BF),
             like((TOKENS, D), BF),
+            like((shards, *attn_slab.shape), BF),
         ],
-        (tokens_here, token_halo, attn_all, by_row, by_lane),
+        (where, tokens_here, token_halo, by_row, by_lane, *pieces),
         scratch=[
             pltpu.VMEM((WINDOWS, WIN, SLOT, D), F32),
             pltpu.VMEM((LANES, PLACES), BF),
             pltpu.VMEM((PLACES, LANES), BF),
             pltpu.VMEM((LANES, FEAT), F32),
             pltpu.VMEM((GROUPS, PLACES, LANES), F32),
+            pltpu.SemaphoreType.DMA((shards,)),
         ],
         flops=5_000_000_000,
-    )
-    out_kept, out_sent, grad_mixed, mlp_grads = kernel_call(
+        smem=1,
+        apart=shards,
+    )
+    out_kept, out_sent, grad_mixed, grad_win, mlp_same, mlp_other = kernel_call(
         mlp_body,
         [
             like((own * WIDTH, D), F32),
             like((SHIFT * WIDTH, D), BF),
             like((TOKENS, D), F32),
-            like(mlp_all.shape, BF),
+            like((PADDED, D), BF),
+            like((chips, 9 * depth + SMALL, D), BF),
+            like((chips, 9 * depth + SMALL, D), BF),
         ],
-        (mixed, cot_here, cot_halo, mlp_all),
+        (where, mixed, cot_here, cot_halo, mlp_all, attn_all, restored),
         scratch=[
             pltpu.VMEM((TOKENS, D), BF),
             pltpu.VMEM((TOKENS, D), BF),
             pltpu.VMEM((TOKENS, D), F32),
             pltpu.VMEM((TOKENS, D), F32),
+            pltpu.VMEM((WINDOWS, WIN, SLOT, D), F32),
         ],
         flops=10_000_000_000,
-    )
-    mlp_share = lax.psum_scatter(mlp_grads, "shard", scatter_dimension=0)
+        smem=1,
+    )
     out_halo = shifted_2(out_sent, "seq", 1)
-    tok_kept, tok_sent, attn_grads = kernel_call(
-        attn_backward_body,
+    scratch = [
+        pltpu.VMEM((LANES, PLACES), BF),
+        pltpu.VMEM((PLACES, LANES), BF),
+        pltpu.VMEM((LANES, FEAT), F32),
+    ]
+    early, pairs_early = kernel_call(
+        attn_first_body,
+        [like((PADDED // 2, 3 * D), BF), like((GROUPS, PLACES, LANES), F32)],
+        (query, key, value, probs, grad_win),
+        scratch=scratch,
+        flops=5_000_000_000,
+    )
+    mlp_sums = add_cores(mlp_same, mlp_other)
+    *mlp_sums, early = lax.optimization_barrier((*mlp_sums, early))
+    tok_kept, tok_sent, attn_same, attn_other = kernel_call(
+        attn_last_body,
         [
             like((own * WIDTH, D), F32),
             like((SHIFT * WIDTH, D), BF),
-            like(attn_all.shape, BF),
+            like((chips, 3 * depth + SMALL, D), BF),
+            like((chips, 3 * depth + SMALL, D), BF),
         ],
         (
+            where,
+            query,
+            key,
+            value,
+            probs,
+            grad_win,
+            early,
+            pairs_early,
             grad_mixed,
             tokens_here,
             token_halo,
             attn_all,
             normed_win,
-            query,
-            key,
-            value,
-            probs,
-            restored,
         ),
         scratch=[
+            pltpu.VMEM((PADDED // 2, 3 * D), BF),
+            *scratch,
+            pltpu.VMEM((GROUPS, PLACES, LANES), F32),
             pltpu.VMEM((WINDOWS, WIN, SLOT, D), F32),
-            pltpu.VMEM((PADDED, 3 * D), BF),
-            pltpu.VMEM((LANES, PLACES), BF),
-            pltpu.VMEM((PLACES, LANES), BF),
-            pltpu.VMEM((LANES, FEAT), F32),
-            pltpu.VMEM((GROUPS, PLACES, LANES), F32),
         ],
         flops=10_000_000_000,
-    )
-    attn_share = lax.psum_scatter(attn_grads, "shard", scatter_dimension=0)
+        smem=1,
+    )
+    mlp_parts = add_chips(where, mlp_sums)
+    mlp_total = add_seq(*mlp_parts)
+    attn_total = add_seq(*add_chips(where, add_cores(attn_same, attn_other)))
     tok_halo = shifted_2(tok_sent, "seq", 1)
-    attn_total, mlp_total = lax.psum((attn_share, mlp_share), "seq")
-    shapes = [like(p.shape, F32) for p in params]
-    summed = kernel_call(unpack_body, shapes, (me, attn_total, mlp_total), smem=1)
+    shapes = [like(p.shape, F32) for p in attn_params + mlp_params]
+    summed = list(
+        kernel_call(
+            unpack_body,
+            shapes,
+            (where, *attn_total, *mlp_total),
+            scratch=[
+                pltpu.VMEM((3 * depth + SMALL, D), BF),
+                pltpu.VMEM((9 * depth + SMALL, D), BF),
+            ],
+            smem=1,
+        )
+    )
+    summed[4] = summed[4].T
 
     def joined(halo, kept):
         return jnp.concatenate([halo.astype(F32), kept], 0).reshape(tokens.shape)
 
-    grads = [s.reshape(p.shape) for s, p in zip(
-        summed,
-        (
-            gain_one,
-            bias_one,
-            w_qkv,
-            bias_qv,
-            table,
-            w_proj,
-            bias_proj,
-            gain_two,
-            bias_two,
-            w_in,
-            bias_in,
-            w_out,
-            bias_out,
-        ),
-    )]
+    targets = (
+        gain_one,
+        bias_one,
+        w_qkv,
+        bias_qv,
+        table,
+        w_proj,
+        bias_proj,
+        gain_two,
+        bias_two,
+        w_in,
+        bias_in,
+        w_out,
+        bias_out,
+    )
+    grads = [g.reshape(p.shape) for g, p in zip(summed, targets)]
     return (joined(out_halo, out_kept), joined(tok_halo, tok_kept), *grads)
 
 

time: 304 us -> 217 us (0.71)
  waiting for transfers between devices: 177 us -> 52.8 us
  Pallas kernels: 93.1 us -> 113 us
  starting transfers between devices: 8.84 us -> 20.3 us
  local copies, waits for them, and re-layouts: 8.24 us -> 12.3 us
    reduce_scatter x2 -> x0, waiting for transfers between devices: 96.7 us -> none  [the longest x1 55.4 us: per_device(): mlp_share = lax.psum_scatter(mlp_grads, 'shard', scatter_dimension=0)]
    ppermute x0 -> x21, waiting for transfers between devices: none -> 49 us  [exchange(): return lax.ppermute(value, axis, [(i, i ^ mask) for i in range(peers)])]
    ppermute x4, waiting for transfers between devices: 36.7 us -> 3.74 us  [shifted_2(): lax.ppermute(value, axis, [(i, (i + by) % peers) for i in range(peers)])]
    psum x1 -> x0, waiting for transfers between devices: 24.1 us -> none  [per_device(): attn_total, mlp_total = lax.psum((attn_share, mlp_share), 'seq')]
    pallas_call x5 -> x11, Pallas kernels: 93.1 us -> 113 us  [kernel_call(): pl.pallas_call(body, out_shape=tuple(outs), in_specs=[whole(pltpu.SMEM)]...]
    ppermute x0 -> x21, starting transfers between devices: none -> 12.1 us  [exchange(): return lax.ppermute(value, axis, [(i, i ^ mask) for i in range(peers)])]
    all_gather x1 -> x0, waiting for transfers between devices: 9.7 us -> none  [per_device(): attn_all = lax.all_gather(attn_slab, 'shard')]
    all_gather x1, waiting for transfers between devices: 8.51 us -> 0.02 us  [per_device(): mlp_all = lax.all_gather(mlp_slab, 'shard')]
  transfers between devices with their start and end apart: 9 -> 26, of which waited for: 8 -> 10; matrix products, arithmetic and copies ran while one was open for 2% -> 3% of each run, Pallas kernels for 10% -> 37%
where the time goes in v2:
time: 217 us; the launch traced here: 216 us
  Pallas kernels  113 us (52%)
  waiting for transfers between devices  52.8 us (24%)
  starting transfers between devices  20.3 us (9%)
  between operations  14.4 us (7%)
  local copies, waits for them, and re-layouts  12.3 us (6%)
  other arithmetic  3.57 us (2%)
    pallas_call x11, Pallas kernels, kernel_call(): pl.pallas_call(body, out_shape=tuple(outs), in_specs=[whole(pltpu.SMEM)]...  113 us
    ppermute x21, waiting for transfers between devices, exchange(): return lax.ppermute(value, axis, [(i, i ^ mask) for i in range(peers)])  49 us
    ppermute x21, starting transfers between devices, exchange(): return lax.ppermute(value, axis, [(i, i ^ mask) for i in range(peers)])  12.1 us
    ppermute x4, starting transfers between devices, shifted_2(): lax.ppermute(value, axis, [(i, (i + by) % peers) for i in range(peers)])  8.09 us
    unnamed x52, local copies, waits for them, and re-layouts  6.92 us
  transfers between devices with their start and end apart: 26, of which 10 were waited for; matrix products, arithmetic and copies ran while one was open for 3% of the time, Pallas kernels for 37%

profile of v2, /device:TPU:0, one launch (start us, length us, event | category | flops | bytes accessed | tf_op | source)
XLA Modules:
  0.0 216.3 jit_solution(1614971945781253765)
XLA Ops:
  7.2 1.2 broadcast_in_dim.43.bin_
  9.1 2.2 %shard_map.273 = bf16[544,512]{1,0:T(8,128)(2,1)} custom-call(s32[2]{0:T(128)} %pad_add_fusion.me_ref, bf16[1,64]{1,0:T(2,128)(2,1)} %bitcast.38, bf16[1,64]{1,0:T(2,128)(2,1)} %bitcast.39, bf16[64,2048]{1,0:T(8,128)(2,1)} %win.1, bf16[1,256]{1,0:T(2,128)(2,1)} %broadcast_in_dim.43.bin_, bf16[256,512]{1,0:T(8,128)(2,1)} %wout.1, bf16[1,64]{1,0:T(2,128)(2,1)} %bitcast.40), custom_call_target="tpu_custom_call" | custom-call | bytes 1082248 | tf_op jit(solution)/shard_map/pallas_call | solution.py:125
  11.3 2.4 %shard_map.271.refs_0_ = bf16[288,512]{1,0:T(8,128)(2,1)} custom-call(s32[2]{0:T(128)} %pad_add_fusion.me_ref, bf16[1,64]{1,0:T(2,128)(2,1)} %bitcast.41, bf16[1,64]{1,0:T(2,128)(2,1)} %bitcast.42, bf16[64,1536]{1,0:T(8,128)(2,1)} %wqkv.1, bf16[2,64]{1,0:T(2,128)(2,1)} %bqv.1, bf16[2,169]{1,0:T(2,128)(2,1)} %bitcast.37, bf16[64,512]{1,0:T(8,128)(2,1)} %wproj.1, ...), custom_call_target="tpu_custom_call" | custom-call | bytes 558380 | tf_op jit(solution)/shard_map/pallas_call | solution.py:125
  13.7 3.9 %collective-permute-start.6 = (bf16[288,512]{1,0:T(8,128)(2,1)}, bf16[288,512]{1,0:T(8,128)(2,1)S(1)}, u32[]{:S(2)}, u32[]{:S(2)}) collective-permute-start(bf16[288,512]{1,0:T(8,128)(2,1)} %shard_map.271.refs_0_), channel_id=1, source_target_pairs={{0,24},{4,28},{8,16},{12,20},{16,8},{20,12},{24,0},{28,4},{1,25},{... | collective-permute-start | bytes 884744 | tf_op jit(solution)/shard_map/ppermute | solution.py:304
  19.1 4.1 %collective-permute-start = (bf16[3,112,512]{2,1,0:T(8,128)(2,1)S(1)}, bf16[3,112,512]{2,1,0:T(8,128)(2,1)S(1)}, u32[]{:S(2)}, u32[]{:S(2)}) collective-permute-start(bf16[3,112,512]{2,1,0:T(8,128)(2,1)S(1)} %slice_bitcast_fusion.1), channel_id=1, source_target_pairs={{0,3},{1,0},{2,1},{3,2},{4,7},{5,4},{6,5},{7,6},{8,11},{9,8},{10,9... | collective-permute-start | bytes 1032200 | tf_op jit(solution)/shard_map/ppermute | solution.py:36
  23.5 4.7 %collective-permute-done.6.refs_6_ = bf16[288,512]{1,0:T(8,128)(2,1)S(1)} collective-permute-done((bf16[288,512]{1,0:T(8,128)(2,1)}, bf16[288,512]{1,0:T(8,128)(2,1)S(1)}, u32[]{:S(2)}, u32[]{:S(2)}) %collective-permute-start.6) | collective-permute-done | bytes 294944 | tf_op jit(solution)/shard_map/ppermute | solution.py:304
  28.2 8.9 %collective-permute-done.4.refs_4_ = bf16[288,512]{1,0:T(8,128)(2,1)S(1)} collective-permute-done((bf16[288,512]{1,0:T(8,128)(2,1)}, bf16[288,512]{1,0:T(8,128)(2,1)S(1)}, u32[]{:S(2)}, u32[]{:S(2)}) %collective-permute-start.4) | collective-permute-done | bytes 294944 | tf_op jit(solution)/shard_map/ppermute | solution.py:304
  39.4 3.8 %collective-permute-start.8 = (bf16[3,112,512]{2,1,0:T(8,128)(2,1)S(1)}, bf16[3,112,512]{2,1,0:T(8,128)(2,1)S(1)}, u32[]{:S(2)}, u32[]{:S(2)}) collective-permute-start(bf16[3,112,512]{2,1,0:T(8,128)(2,1)S(1)} %slice_bitcast_fusion), channel_id=1, source_target_pairs={{0,3},{1,0},{2,1},{3,2},{4,7},{5,4},{6,5},{7,6},{8,11},{9,8},{10,9... | collective-permute-start | bytes 1032200 | tf_op jit(solution)/shard_map/ppermute | solution.py:36
  43.4 1.1 broadcast_in_dim.35.reg_rows
  44.5 31.8 %shard_map.272 = (f32[784,512]{1,0:T(8,128)}, bf16[896,512]{1,0:T(8,128)(2,1)}, bf16[896,512]{1,0:T(8,128)(2,1)}, bf16[896,512]{1,0:T(8,128)(2,1)}, bf16[896,512...) custom-call(s32[2]{0:T(128)} %pad_add_fusion.me_ref, ...), custom_call_target="tpu_custom_call" | custom-call | flops 5000000000 | bytes 14270472 | tf_op jit(solution)/shard_map/pallas_call | solution.py:125
  77.0 24.1 %shard_map.274 = (f32[448,512]{1,0:T(8,128)}, bf16[336,512]{1,0:T(8,128)(2,1)}, f32[784,512]{1,0:T(8,128)}, bf16[896,512]{1,0:T(8,128)(2,1)}, bf16[4,608,512]{2,...) custom-call(s32[2]{0:T(128)} %pad_add_fusion.me_ref, f32[784,512]{1,0:T(8,128)} %get-tuple-element.65.mixed, ...), custom_call_target="tpu_custom_call" | custom-call | flops 10000000000 | bytes 19136520 | tf_op jit(solution)/shard_map/pallas_call | solution.py:125
  101.1 15.1 %shard_map.276 = (bf16[448,1536]{1,0:T(8,128)(2,1)}, f32[2,56,512]{2,1,0:T(8,128)}) custom-call(bf16[896,512]{1,0:T(8,128)(2,1)} %get-tuple-element.70.query, bf16[896,512]{1,0:T(8,128)(2,1)} %get-tuple-element.71.key, bf16[896,512]{1,0:T(8,128)(2,1)} %get-tuple-element.72.value, bf16[8,2,112,512]{3,2,1,0:T(8,128)(2,1)} %get-tuple-element.73.probs, ...), custom_call_target="tpu_custom_call" | custom-call | flops 5000000000 | bytes 7110656 | tf_op jit(solution)/shard_map/pallas_call | solution.py:125
  116.3 1.5 copy-done.1
  117.7 4.1 %shard_map.275 = (bf16[608,512]{1,0:T(8,128)(2,1)}, bf16[608,512]{1,0:T(8,128)(2,1)}, bf16[608,512]{1,0:T(8,128)(2,1)}, bf16[608,512]{1,0:T(8,128)(2,1)}) custom-call(bf16[4,608,512]{2,1,0:T(8,128)(2,1)} %get-tuple-element.75.same, bf16[4,608,512]{2,1,0:T(8,128)(2,1)} %copy-done.1), custom_call_target="tpu_custom_call" | custom-call | bytes 7471104 | tf_op jit(solution)/shard_map/pallas_call | solution.py:125
  121.8 1.5 collective-permute-start.19
  124.2 1.1 collective-permute-start.21
  125.3 22.9 %shard_map.277 = (f32[448,512]{1,0:T(8,128)}, bf16[336,512]{1,0:T(8,128)(2,1)}, bf16[4,224,512]{2,1,0:T(8,128)(2,1)}, bf16[4,224,512]{2,1,0:T(8,128)(2,1)}) custom-call(s32[2]{0:T(128)} %pad_add_fusion.me_ref, bf16[896,512]{1,0:T(8,128)(2,1)} %get-tuple-element.70.query, bf16[896,512]{1,0:T(8,128)(2,1)} %get-tuple-element.71.key, ...), custom_call_target="tpu_custom_call" | custom-call | flops 10000000000 | bytes 16236552 | tf_op jit(solution)/shard_map/pallas_call | solution.py:125
  148.3 4.7 %collective-permute-done.20.refs_2_ = bf16[608,512]{1,0:T(8,128)(2,1)S(1)} collective-permute-done((bf16[608,512]{1,0:T(8,128)(2,1)}, bf16[608,512]{1,0:T(8,128)(2,1)S(1)}, u32[]{:S(2)}, u32[]{:S(2)}) %collective-permute-start.20) | collective-permute-done | bytes 622624 | tf_op jit(solution)/shard_map/ppermute | solution.py:304
  154.7 2.7 %shard_map.280 = (bf16[304,512]{1,0:T(8,128)(2,1)}, bf16[304,512]{1,0:T(8,128)(2,1)}) custom-call(s32[2]{0:T(128)} %pad_add_fusion.me_ref, bf16[608,512]{1,0:T(8,128)(2,1)} %get-tuple-element.96.refs_0_, bf16[608,512]{1,0:T(8,128)(2,1)} %copy-done.6, bf16[608,512]{1,0:T(8,128)(2,1)} %copy-done.7, bf16[608,512]{1,0:T(8,128)(2,1)} %copy-done.8), custom_call_target="tpu_custom_call" | custom-call | bytes 3112968 | tf_op jit(solution)/shard_map/pallas_call | solution.py:125
  157.4 3.7 %collective-permute-done.9 = bf16[336,512]{1,0:T(8,128)(2,1)S(1)} collective-permute-done((bf16[336,512]{1,0:T(8,128)(2,1)}, bf16[336,512]{1,0:T(8,128)(2,1)S(1)}, u32[]{:S(2)}, u32[]{:S(2)}) %collective-permute-start.9) | collective-permute-done | bytes 344096 | tf_op jit(solution)/shard_map/ppermute | solution.py:36
  162.2 2.5 %shard_map.278 = (bf16[224,512]{1,0:T(8,128)(2,1)}, bf16[224,512]{1,0:T(8,128)(2,1)}, bf16[224,512]{1,0:T(8,128)(2,1)}, bf16[224,512]{1,0:T(8,128)(2,1)}) custom-call(bf16[4,224,512]{2,1,0:T(8,128)(2,1)} %get-tuple-element.88.same, bf16[4,224,512]{2,1,0:T(8,128)(2,1)} %copy-done.3), custom_call_target="tpu_custom_call" | custom-call | bytes 2752512 | tf_op jit(solution)/shard_map/pallas_call | solution.py:125
  164.8 1.5 collective-permute-start.13
  167.1 1.1 collective-permute-start.15
  168.6 4.9 %collective-permute-done.13.refs_1_ = bf16[224,512]{1,0:T(8,128)(2,1)S(1)} collective-permute-done((bf16[224,512]{1,0:T(8,128)(2,1)}, bf16[224,512]{1,0:T(8,128)(2,1)S(1)}, u32[]{:S(2)}, u32[]{:S(2)}) %collective-permute-start.13) | collective-permute-done | bytes 229408 | tf_op jit(solution)/shard_map/ppermute | solution.py:304
  173.5 4.3 %collective-permute-done.14.refs_2_ = bf16[224,512]{1,0:T(8,128)(2,1)S(1)} collective-permute-done((bf16[224,512]{1,0:T(8,128)(2,1)}, bf16[224,512]{1,0:T(8,128)(2,1)S(1)}, u32[]{:S(2)}, u32[]{:S(2)}) %collective-permute-start.14) | collective-permute-done | bytes 229408 | tf_op jit(solution)/shard_map/ppermute | solution.py:304
  178.6 2.1 shard_map.279
  180.7 1.3 pad_maximum_fusion
  182.0 8.5 %collective-permute-done.16 = bf16[112,512]{1,0:T(8,128)(2,1)S(1)} collective-permute-done((bf16[112,512]{1,0:T(8,128)(2,1)}, bf16[112,512]{1,0:T(8,128)(2,1)S(1)}, u32[]{:S(2)}, u32[]{:S(2)}) %collective-permute-start.16) | collective-permute-done | bytes 114720 | tf_op jit(solution)/shard_map/ppermute | solution.py:304
  190.8 7.4 %collective-permute-done.17 = bf16[112,512]{1,0:T(8,128)(2,1)S(1)} collective-permute-done((bf16[112,512]{1,0:T(8,128)(2,1)S(1)}, bf16[112,512]{1,0:T(8,128)(2,1)S(1)}, u32[]{:S(2)}, u32[]{:S(2)}) %collective-permute-start.17) | collective-permute-done | bytes 114720 | tf_op jit(solution)/shard_map/ppermute | solution.py:304
  198.3 1.3 pad_maximum_fusion.1
  199.6 5.3 %collective-permute-done.18.attn_back = bf16[112,512]{1,0:T(8,128)(2,1)S(1)} collective-permute-done((bf16[112,512]{1,0:T(8,128)(2,1)S(1)}, bf16[112,512]{1,0:T(8,128)(2,1)S(1)}, u32[]{:S(2)}, u32[]{:S(2)}) %collective-permute-start.18) | collective-permute-done | bytes 114720 | tf_op jit(solution)/shard_map/ppermute | solution.py:304
  206.3 3.1 %shard_map.281 = (f32[1,64]{1,0:T(1,128)}, f32[1,64]{1,0:T(1,128)}, f32[64,1536]{1,0:T(8,128)}, f32[2,64]{1,0:T(2,128)}, f32[2,169]{1,0:T(2,128)}, /*index=5*/f3...) custom-call(s32[2]{0:T(128)} %pad_add_fusion.me_ref, ...), custom_call_target="tpu_custom_call" | custom-call | bytes 2429264 | tf_op jit(solution)/shard_map/pallas_call | solution.py:125
  (106 shorter events, 13.0 us)
Async XLA Ops:
  7.2 16.1 %copy-start = (s32[1,28,112]{2,0,1:T(1,128)S(1)}, s32[1,28,112]{2,0,1:T(1,128)}, u32[]{:S(2)}) copy-start(s32[1,28,112]{2,0,1:T(1,128)} %param.17) | copy-start | bytes 37636
  7.2 69.1 %all-gather.3.cloned.1.call-start = ((), (), s32[]{:S(2)}) async-start(), calls=%async_computation | async-start | bytes 5013504 | tf_op jit(solution)/shard_map/all_gather | solution.py:738
  13.7 14.5 %collective-permute-start.6 = (bf16[288,512]{1,0:T(8,128)(2,1)}, bf16[288,512]{1,0:T(8,128)(2,1)S(1)}, u32[]{:S(2)}, u32[]{:S(2)}) collective-permute-start(bf16[288,512]{1,0:T(8,128)(2,1)} %shard_map.271.refs_0_), channel_id=1, source_target_pairs={{0,24},{4,28},{8,16},{12,20},{16,8},{20,12},{24,0},{28,4},{1,25},{... | collective-permute-start | bytes 884744 | tf_op jit(solution)/shard_map/ppermute | solution.py:304
  17.6 19.5 %collective-permute-start.4 = (bf16[288,512]{1,0:T(8,128)(2,1)}, bf16[288,512]{1,0:T(8,128)(2,1)S(1)}, u32[]{:S(2)}, u32[]{:S(2)}) collective-permute-start(bf16[288,512]{1,0:T(8,128)(2,1)} %shard_map.271.refs_0_), channel_id=1, source_target_pairs={{0,16},{4,20},{8,24},{12,28},{16,0},{20,4},{24,8},{28,12},{1,17},{... | collective-permute-start | bytes 884744 | tf_op jit(solution)/shard_map/ppermute | solution.py:304
  18.1 19.3 %collective-permute-start.2 = (bf16[288,512]{1,0:T(8,128)(2,1)}, bf16[288,512]{1,0:T(8,128)(2,1)S(1)}, u32[]{:S(2)}, u32[]{:S(2)}) collective-permute-start(bf16[288,512]{1,0:T(8,128)(2,1)} %shard_map.271.refs_0_), channel_id=1, source_target_pairs={{0,8},{4,12},{8,0},{12,4},{16,24},{20,28},{24,16},{28,20},{1,9},{5... | collective-permute-start | bytes 884744 | tf_op jit(solution)/shard_map/ppermute | solution.py:304
  18.1 21.3 %collective-permute-start.1 = (bf16[288,512]{1,0:T(8,128)(2,1)}, bf16[288,512]{1,0:T(8,128)(2,1)S(1)}, u32[]{:S(2)}, u32[]{:S(2)}) collective-permute-start(bf16[288,512]{1,0:T(8,128)(2,1)} %shard_map.271.refs_0_), channel_id=1, source_target_pairs={{0,4},{4,0},{8,12},{12,8},{16,20},{20,16},{24,28},{28,24},{1,5},{5... | collective-permute-start | bytes 884744 | tf_op jit(solution)/shard_map/ppermute | solution.py:304
  19.1 24.2 %collective-permute-start = (bf16[3,112,512]{2,1,0:T(8,128)(2,1)S(1)}, bf16[3,112,512]{2,1,0:T(8,128)(2,1)S(1)}, u32[]{:S(2)}, u32[]{:S(2)}) collective-permute-start(bf16[3,112,512]{2,1,0:T(8,128)(2,1)S(1)} %slice_bitcast_fusion.1), channel_id=1, source_target_pairs={{0,3},{1,0},{2,1},{3,2},{4,7},{5,4},{6,5},{7,6},{8,11},{9,8},{10,9... | collective-permute-start | bytes 1032200 | tf_op jit(solution)/shard_map/ppermute | solution.py:36
  28.2 16.3 %copy-start.19 = (bf16[288,512]{1,0:T(8,128)(2,1)}, bf16[288,512]{1,0:T(8,128)(2,1)S(1)}, u32[]{:S(2)}) copy-start(bf16[288,512]{1,0:T(8,128)(2,1)S(1)} %collective-permute-done.6.refs_6_) | copy-start | bytes 884740
  28.2 15.1 %collective-permute-start.7 = (bf16[288,512]{1,0:T(8,128)(2,1)S(1)}, bf16[288,512]{1,0:T(8,128)(2,1)S(1)}, u32[]{:S(2)}, u32[]{:S(2)}) collective-permute-start(bf16[288,512]{1,0:T(8,128)(2,1)S(1)} %collective-permute-done.6.refs_6_), channel_id=1, source_target_pairs={{0,4},{4,0},{8,12},{12,8},{16,20},{20,16},{24,28},{28,24},{1,5},{5... | collective-permute-start | bytes 884744 | tf_op jit(solution)/shard_map/ppermute | solution.py:304
  37.1 6.3 %collective-permute-start.5 = (bf16[288,512]{1,0:T(8,128)(2,1)S(1)}, bf16[288,512]{1,0:T(8,128)(2,1)S(1)}, u32[]{:S(2)}, u32[]{:S(2)}) collective-permute-start(bf16[288,512]{1,0:T(8,128)(2,1)S(1)} %collective-permute-done.4.refs_4_), channel_id=1, source_target_pairs={{0,4},{4,0},{8,12},{12,8},{16,20},{20,16},{24,28},{28,24},{1,5},{5... | collective-permute-start | bytes 884744 | tf_op jit(solution)/shard_map/ppermute | solution.py:304
  37.4 6.0 %collective-permute-start.3 = (bf16[288,512]{1,0:T(8,128)(2,1)S(1)}, bf16[288,512]{1,0:T(8,128)(2,1)S(1)}, u32[]{:S(2)}, u32[]{:S(2)}) collective-permute-start(bf16[288,512]{1,0:T(8,128)(2,1)S(1)} %collective-permute-done.2.refs_2_), channel_id=1, source_target_pairs={{0,4},{4,0},{8,12},{12,8},{16,20},{20,16},{24,28},{28,24},{1,5},{5... | collective-permute-start | bytes 884744 | tf_op jit(solution)/shard_map/ppermute | solution.py:304
  39.4 36.9 %collective-permute-start.8 = (bf16[3,112,512]{2,1,0:T(8,128)(2,1)S(1)}, bf16[3,112,512]{2,1,0:T(8,128)(2,1)S(1)}, u32[]{:S(2)}, u32[]{:S(2)}) collective-permute-start(bf16[3,112,512]{2,1,0:T(8,128)(2,1)S(1)} %slice_bitcast_fusion), channel_id=1, source_target_pairs={{0,3},{1,0},{2,1},{3,2},{4,7},{5,4},{6,5},{7,6},{8,11},{9,8},{10,9... | collective-permute-start | bytes 1032200 | tf_op jit(solution)/shard_map/ppermute | solution.py:36
  101.1 15.1 %collective-permute-start.10 = (bf16[4,608,512]{2,1,0:T(8,128)(2,1)}, bf16[4,608,512]{2,1,0:T(8,128)(2,1)S(1)}, u32[]{:S(2)}, u32[]{:S(2)}) collective-permute-start(bf16[4,608,512]{2,1,0:T(8,128)(2,1)} %get-tuple-element.76), channel_id=1, source_target_pairs={{0,4},{4,0},{8,12},{12,8},{16,20},{20,16},{24,28},{28,24},{1,5},{5... | collective-permute-start | bytes 7471112 | tf_op jit(solution)/shard_map/ppermute | solution.py:304
  121.8 26.5 %collective-permute-start.19 = (bf16[608,512]{1,0:T(8,128)(2,1)}, bf16[608,512]{1,0:T(8,128)(2,1)S(1)}, u32[]{:S(2)}, u32[]{:S(2)}) collective-permute-start(bf16[608,512]{1,0:T(8,128)(2,1)} %get-tuple-element.97), channel_id=1, source_target_pairs={{0,8},{4,12},{8,0},{12,4},{16,24},{20,28},{24,16},{28,20},{1,9},{5... | collective-permute-start | bytes 1867784 | tf_op jit(solution)/shard_map/ppermute | solution.py:304
  123.3 29.7 %collective-permute-start.20 = (bf16[608,512]{1,0:T(8,128)(2,1)}, bf16[608,512]{1,0:T(8,128)(2,1)S(1)}, u32[]{:S(2)}, u32[]{:S(2)}) collective-permute-start(bf16[608,512]{1,0:T(8,128)(2,1)} %get-tuple-element.98), channel_id=1, source_target_pairs={{0,16},{4,20},{8,24},{12,28},{16,0},{20,4},{24,8},{28,12},{1,17},{... | collective-permute-start | bytes 1867784 | tf_op jit(solution)/shard_map/ppermute | solution.py:304
  124.2 28.8 %collective-permute-start.21 = (bf16[608,512]{1,0:T(8,128)(2,1)}, bf16[608,512]{1,0:T(8,128)(2,1)S(1)}, u32[]{:S(2)}, u32[]{:S(2)}) collective-permute-start(bf16[608,512]{1,0:T(8,128)(2,1)} %get-tuple-element.99), channel_id=1, source_target_pairs={{0,24},{4,28},{8,16},{12,20},{16,8},{20,12},{24,0},{28,4},{1,25},{... | collective-permute-start | bytes 1867784 | tf_op jit(solution)/shard_map/ppermute | solution.py:304
  148.2 13.1 %collective-permute-start.12 = (bf16[4,224,512]{2,1,0:T(8,128)(2,1)}, bf16[4,224,512]{2,1,0:T(8,128)(2,1)S(1)}, u32[]{:S(2)}, u32[]{:S(2)}) collective-permute-start(bf16[4,224,512]{2,1,0:T(8,128)(2,1)} %get-tuple-element.89), channel_id=1, source_target_pairs={{0,4},{4,0},{8,12},{12,8},{16,20},{20,16},{24,28},{28,24},{1,5},{5... | collective-permute-start | bytes 2752520 | tf_op jit(solution)/shard_map/ppermute | solution.py:304
  148.2 12.9 %collective-permute-start.9 = (bf16[336,512]{1,0:T(8,128)(2,1)}, bf16[336,512]{1,0:T(8,128)(2,1)S(1)}, u32[]{:S(2)}, u32[]{:S(2)}) collective-permute-start(bf16[336,512]{1,0:T(8,128)(2,1)} %get-tuple-element.68), channel_id=1, source_target_pairs={{0,1},{1,2},{2,3},{3,0},{4,5},{5,6},{6,7},{7,4},{8,9},{9,10},{10,1... | collective-permute-start | bytes 1032200 | tf_op jit(solution)/shard_map/ppermute | solution.py:36
  157.4 10.8 %copy-start.10 = (bf16[304,512]{1,0:T(8,128)(2,1)S(1)}, bf16[304,512]{1,0:T(8,128)(2,1)}, u32[]{:S(2)}) copy-start(bf16[304,512]{1,0:T(8,128)(2,1)} %get-tuple-element.100) | copy-start | bytes 933892
  157.4 10.8 %collective-permute-start.22 = (bf16[304,512]{1,0:T(8,128)(2,1)}, bf16[304,512]{1,0:T(8,128)(2,1)S(1)}, u32[]{:S(2)}, u32[]{:S(2)}) collective-permute-start(bf16[304,512]{1,0:T(8,128)(2,1)} %get-tuple-element.101), channel_id=1, source_target_pairs={{0,1},{1,0},{2,3},{3,2},{4,5},{5,4},{6,7},{7,6},{8,9},{9,8},{10,11... | collective-permute-start | bytes 933896 | tf_op jit(solution)/shard_map/ppermute | solution.py:304
  161.2 20.7 %collective-permute-start.11 = (bf16[336,512]{1,0:T(8,128)(2,1)}, bf16[336,512]{1,0:T(8,128)(2,1)S(1)}, u32[]{:S(2)}, u32[]{:S(2)}) collective-permute-start(bf16[336,512]{1,0:T(8,128)(2,1)} %get-tuple-element.86), channel_id=1, source_target_pairs={{0,1},{1,2},{2,3},{3,0},{4,5},{5,6},{6,7},{7,4},{8,9},{9,10},{10,1... | collective-permute-start | bytes 1032200 | tf_op jit(solution)/shard_map/ppermute | solution.py:36
  162.2 18.4 %copy-start.4 = (f32[448,512]{1,0:T(8,128)S(1)}, f32[448,512]{1,0:T(8,128)}, u32[]{:S(2)}) copy-start(f32[448,512]{1,0:T(8,128)} %get-tuple-element.69) | copy-start | bytes 2752516
  164.8 8.8 %collective-permute-start.13 = (bf16[224,512]{1,0:T(8,128)(2,1)}, bf16[224,512]{1,0:T(8,128)(2,1)S(1)}, u32[]{:S(2)}, u32[]{:S(2)}) collective-permute-start(bf16[224,512]{1,0:T(8,128)(2,1)} %get-tuple-element.91), channel_id=1, source_target_pairs={{0,8},{4,12},{8,0},{12,4},{16,24},{20,28},{24,16},{28,20},{1,9},{5... | collective-permute-start | bytes 688136 | tf_op jit(solution)/shard_map/ppermute | solution.py:304
  166.3 11.6 %collective-permute-start.14 = (bf16[224,512]{1,0:T(8,128)(2,1)}, bf16[224,512]{1,0:T(8,128)(2,1)S(1)}, u32[]{:S(2)}, u32[]{:S(2)}) collective-permute-start(bf16[224,512]{1,0:T(8,128)(2,1)} %get-tuple-element.92), channel_id=1, source_target_pairs={{0,16},{4,20},{8,24},{12,28},{16,0},{20,4},{24,8},{28,12},{1,17},{... | collective-permute-start | bytes 688136 | tf_op jit(solution)/shard_map/ppermute | solution.py:304
  167.1 10.7 %collective-permute-start.15 = (bf16[224,512]{1,0:T(8,128)(2,1)}, bf16[224,512]{1,0:T(8,128)(2,1)S(1)}, u32[]{:S(2)}, u32[]{:S(2)}) collective-permute-start(bf16[224,512]{1,0:T(8,128)(2,1)} %get-tuple-element.93), channel_id=1, source_target_pairs={{0,24},{4,28},{8,16},{12,20},{16,8},{20,12},{24,0},{28,4},{1,25},{... | collective-permute-start | bytes 688136 | tf_op jit(solution)/shard_map/ppermute | solution.py:304
  168.3 22.3 %collective-permute-start.23 = (bf16[304,512]{1,0:T(8,128)(2,1)S(1)}, bf16[304,512]{1,0:T(8,128)(2,1)S(1)}, u32[]{:S(2)}, u32[]{:S(2)}) collective-permute-start(bf16[304,512]{1,0:T(8,128)(2,1)S(1)} %add_convert_fusion.1), channel_id=1, source_target_pairs={{0,2},{1,3},{2,0},{3,1},{4,6},{5,7},{6,4},{7,5},{8,10},{9,11},{10,... | collective-permute-start | bytes 933896 | tf_op jit(solution)/shard_map/ppermute | solution.py:304
  180.6 9.9 %collective-permute-start.16 = (bf16[112,512]{1,0:T(8,128)(2,1)}, bf16[112,512]{1,0:T(8,128)(2,1)S(1)}, u32[]{:S(2)}, u32[]{:S(2)}) collective-permute-start(bf16[112,512]{1,0:T(8,128)(2,1)} %get-tuple-element.95), channel_id=1, source_target_pairs={{0,1},{1,0},{2,3},{3,2},{4,5},{5,4},{6,7},{7,6},{8,9},{9,8},{10,11... | collective-permute-start | bytes 344072 | tf_op jit(solution)/shard_map/ppermute | solution.py:304
  180.7 9.9 %copy-start.16 = (bf16[112,512]{1,0:T(8,128)(2,1)S(1)}, bf16[112,512]{1,0:T(8,128)(2,1)}, u32[]{:S(2)}) copy-start(bf16[112,512]{1,0:T(8,128)(2,1)} %get-tuple-element.94) | copy-start | bytes 344068
  181.9 16.4 %copy-start.5 = (f32[448,512]{1,0:T(8,128)S(1)}, f32[448,512]{1,0:T(8,128)}, u32[]{:S(2)}) copy-start(f32[448,512]{1,0:T(8,128)} %get-tuple-element.87) | copy-start | bytes 2752516
  190.5 7.6 %collective-permute-start.17 = (bf16[112,512]{1,0:T(8,128)(2,1)S(1)}, bf16[112,512]{1,0:T(8,128)(2,1)S(1)}, u32[]{:S(2)}, u32[]{:S(2)}) collective-permute-start(bf16[112,512]{1,0:T(8,128)(2,1)S(1)} %add_convert_fusion.3), channel_id=1, source_target_pairs={{0,2},{1,3},{2,0},{3,1},{4,6},{5,7},{6,4},{7,5},{8,10},{9,11},{10,... | collective-permute-start | bytes 344072 | tf_op jit(solution)/shard_map/ppermute | solution.py:304
  190.7 14.2 %collective-permute-start.24 = (bf16[304,512]{1,0:T(8,128)(2,1)S(1)}, bf16[304,512]{1,0:T(8,128)(2,1)S(1)}, u32[]{:S(2)}, u32[]{:S(2)}) collective-permute-start(bf16[304,512]{1,0:T(8,128)(2,1)S(1)} %add_convert_fusion.mlp_half), channel_id=1, source_target_pairs={{0,1},{1,0},{2,3},{3,2},{4,5},{5,4},{6,7},{7,6},{8,9},{9,8},{10,11... | collective-permute-start | bytes 933896 | tf_op jit(solution)/shard_map/ppermute | solution.py:304
  198.2 6.7 %collective-permute-start.18 = (bf16[112,512]{1,0:T(8,128)(2,1)S(1)}, bf16[112,512]{1,0:T(8,128)(2,1)S(1)}, u32[]{:S(2)}, u32[]{:S(2)}) collective-permute-start(bf16[112,512]{1,0:T(8,128)(2,1)S(1)} %add_convert_fusion.2.attn_half), channel_id=1, source_target_pairs={{0,1},{1,0},{2,3},{3,2},{4,5},{5,4},{6,7},{7,6},{8,9},{9,8},{10,11... | collective-permute-start | bytes 344072 | tf_op jit(solution)/shard_map/ppermute | solution.py:304
  (20 other events, 51.3 us)
Sparse Core Ops, SparseCore 0:
  11.4 47.5 all-gather.2
